TPU v7x, 512 devices: a whole 4x8x8 slice. The times are simulated.
512 devices in a mesh: genome: 128 (over y, z, core), rep: 4 (over x).
Axes of the slice: x: 4, y: 8, z: 8, core: 2. Of those that a mesh axis runs over, the one named last changes fastest.
Arguments:
- band_tiles: float32 [1024, 5, 256, 256], P(('genome', 'rep'))
- trans_tiles: float32 [3072, 256, 256], P(('genome', 'rep'))
- trans_rows: int32 [3072], P(('genome', 'rep')), may hold values from 0 to 1023
- trans_cols: int32 [3072], P(('genome', 'rep')), may hold values from 0 to 1023
- trans_count: int32 [512], P(('genome', 'rep')), may hold values from 0 to 6, as said below
- masked: int32 [262144], P('genome'), may hold values 0 or 1
Outputs:
- weights: float32 [262144], P('genome')
- coverage: float32 [262144], P('genome')
Inputs may be any that keep to these rules, and one draw needn't show every extreme that they name: `trans_count`: for device d = g * 4 + r, its used slots have row blocks within g * 8 to (g + 1) * 8 - 1 and column blocks on distinct genome indices of g + 2 or more; the device g = 0, r = 0 uses all 6 slots.
All inputs are finite; a program needn't handle non-finite values. No bound on the sum of `masked` on one device may be relied on, other than what follows from the above.
Results may differ from a plain program's by a relative error of at most 0.00012.
Values sent between devices are 32-bit elements; how exact they have to be, the bound alone decides.
No kernel may reach another device: no remote copies, remote signals or barrier semaphores. Data moves between devices by JAX's collectives and lax.ppermute only.
A program may use at most 128 MiB of HBM per device.

v0:
```python
import jax
import jax.numpy as jnp
from jax import lax
from jax.sharding import PartitionSpec as P

ITERS = 2


HIGH = lax.Precision.HIGHEST


def shifted(block, axis, distance):
    devices = range(lax.axis_size(axis))
    route = [(i - distance, i) for i in devices if i - distance in devices]
    return lax.ppermute(block, axis, route)


def shards(band_tiles, trans_tiles, trans_rows, trans_cols, trans_count, masked):
    blk_dev = band_tiles.shape[0]
    span_count = band_tiles.shape[1]
    reach_blocks = span_count - 1
    width_bins = band_tiles.shape[2]
    replicas = lax.axis_size("rep")
    replica_at = lax.axis_index("rep")
    groups = lax.axis_size("genome")
    genome_at = lax.axis_index("genome")
    blk_g = blk_dev * replicas
    all_blocks = blk_g * groups
    unmasked = (1 - masked).astype(jnp.float32).reshape(blk_g, width_bins)
    upper = jnp.triu(jnp.ones((width_bins, width_bins), jnp.float32))
    offset_ids = jnp.arange(span_count)
    shape_mask = jnp.where(
        offset_ids[:, None, None] == 0,
        upper[None],
        jnp.ones((1, width_bins, width_bins), jnp.float32),
    )
    diagonal_zero = jnp.diagonal(band_tiles[:, 0], axis1=1, axis2=2)
    tile_count = trans_tiles.shape[0]
    active = (jnp.arange(tile_count, dtype=jnp.int32) < trans_count[0]).astype(jnp.float32)
    local_rows = trans_rows - genome_at * blk_g
    row_hot = (local_rows[:, None] == jnp.arange(blk_g, dtype=jnp.int32)[None]).astype(
        jnp.float32
    ) * active[:, None]
    col_hot = (trans_cols[:, None] == jnp.arange(all_blocks, dtype=jnp.int32)[None]).astype(
        jnp.float32
    ) * active[:, None]
    anchor = replica_at * blk_dev
    reach = anchor + jnp.arange(blk_dev)[:, None] + jnp.arange(span_count)[None, :]
    own_rows = anchor + jnp.arange(blk_dev)
    weights = unmasked
    coverage = unmasked
    for sweep in range(ITERS):
        forward = shifted(weights[:reach_blocks], "genome", -1)
        extended = jnp.concatenate([weights, forward], axis=0)
        column_bias = extended[reach]
        row_bias = lax.dynamic_slice_in_dim(weights, anchor, blk_dev, 0)
        masked_tiles = band_tiles * shape_mask[None]
        row_terms = row_bias * jnp.einsum("qkij,qkj->qi", masked_tiles, column_bias, precision=HIGH)
        row_terms = row_terms - row_bias * row_bias * diagonal_zero
        col_terms = column_bias * jnp.einsum("qkij,qi->qkj", masked_tiles, row_bias, precision=HIGH)
        partial_value = jnp.zeros((blk_g + reach_blocks, width_bins), jnp.float32)
        partial_value = partial_value.at[own_rows].add(row_terms)
        partial_value = partial_value.at[reach.reshape(-1)].add(col_terms.reshape(-1, width_bins))
        trans_row_bias = jnp.dot(row_hot, weights, precision=HIGH)
        every_bias = lax.all_gather(weights, "genome", axis=0, tiled=True)
        trans_col_bias = jnp.dot(col_hot, every_bias, precision=HIGH)
        trans_row = trans_row_bias * jnp.einsum(
            "tij,tj->ti", trans_tiles, trans_col_bias, precision=HIGH
        )
        trans_col = trans_col_bias * jnp.einsum(
            "tij,ti->tj", trans_tiles, trans_row_bias, precision=HIGH
        )
        local_sums = jnp.dot(row_hot.T, trans_row, precision=HIGH)
        spread = jnp.dot(col_hot.T, trans_col, precision=HIGH)
        returned = lax.psum_scatter(spread, "genome", scatter_dimension=0, tiled=True)
        partial_value = partial_value.at[:blk_g].add(local_sums + returned)
        summed = lax.psum(partial_value, "rep")
        spill = shifted(summed[blk_g:], "genome", 1)
        coverage = summed[:blk_g].at[:reach_blocks].add(spill)
        bin_total, bin_count = lax.psum((jnp.sum(coverage * unmasked), jnp.sum(unmasked)), "genome")
        average = bin_total / bin_count
        weights = unmasked * weights / jnp.where(unmasked > 0, coverage / average, 1.0)
    return (weights.reshape(-1), coverage.reshape(-1))


def solution(mesh):
    in_specs = (
        P(("genome", "rep"), None, None, None),
        P(("genome", "rep"), None, None),
        P(("genome", "rep")),
        P(("genome", "rep")),
        P(("genome", "rep")),
        P("genome"),
    )
    out_specs = (P("genome"), P("genome"))
    return jax.shard_map(shards, mesh=mesh, in_specs=in_specs, out_specs=out_specs, check_vma=False)
```

profile of v0, /device:TPU:1, one launch (start us, length us, event | category | flops | bytes accessed | tf_op | source)
XLA Modules:
  0.0 1118.7 jit_solution(11206024954920251752)
XLA Ops:
  7.2 0.0 copy-start
  7.2 0.0 all-gather.3.cloned.1.call-start
  7.2 0.8 subtract_convert_fusion
  8.1 8.8 collective-permute-start
  16.8 0.6 reshape.239
  17.4 0.0 all-gather.3.cloned.1.call-update
  17.5 0.0 reduce-scatter.3.cloned.1.call-start
  17.5 0.1 compare_select_fusion
  17.6 0.1 reshape.246
  17.7 0.1 iota_add_fusion
  17.8 0.1 add.182
  18.5 0.7 fusion.83
  19.3 0.7 broadcast_subtract_fusion
  19.9 0.9 fusion.49
  20.8 0.1 fusion.16
  20.9 0.2 broadcast_select_fusion
  21.1 0.9 fusion.55
  22.0 74.8 %all-gather.3.cloned.1.call-done = f32[1024,256]{1,0:T(8,128)} async-done(((f32[8,256]{1,0:T(8,128)}), f32[1024,256]{1,0:T(8,128)}) %all-gather.3.cloned.1.call-update) | async-done | bytes 1048592 | tf_op jit(solution)/shard_map/all_gather | solution.py:65
  96.8 1.8 fusion.23
  98.6 2.1 fusion.21
  100.7 0.0 reduce-scatter.3.cloned.1.call-update
  100.7 0.0 all-gather.5.cloned.1.call-start
  100.8 3.3 fusion.4
  104.2 16.5 %copy.28 = f32[2,1,256,256]{0,3,2,1:T(8,128)} copy(f32[2,1,256,256]{3,2,1,0:T(8,128)S(1)} %slice-done) | data formatting | bytes 1048576
  120.7 2.4 gather_fusion.1
  123.0 0.1 copy.11
  123.1 0.6 gather_fusion
  123.7 4.1 fusion.6
  127.9 0.6 scatter_custom_fusion
  128.5 0.7 scatter_fusion
  129.2 1.4 fusion.57
  130.6 159.5 %reduce-scatter.3.cloned.1.call-done = f32[8,256]{1,0:T(8,128)} async-done(((f32[1024,256]{1,0:T(8,128)}), f32[8,256]{1,0:T(8,128)}) %reduce-scatter.3.cloned.1.call-update) | async-done | bytes 8208 | tf_op jit(solution)/shard_map/reduce_scatter | solution.py:75
  290.1 1.0 fusion.15
  291.0 13.1 %psum.38 = f32[12,256]{1,0:T(8,128)S(1)} all-reduce(f32[12,256]{1,0:T(8,128)S(1)} %fusion.15), channel_id=1, replica_groups=mesh['genome'=128,'rep'=4] {'rep'}, use_global_device_ids=true, to_apply=%region_3.4 | all-reduce | flops 3072 | bytes 24576 | tf_op jit(solution)/shard_map/psum | solution.py:77
  304.1 11.3 %collective-permute-start.1 = (f32[4,256]{1,0:T(4,128)S(1)}, f32[4,256]{1,0:T(4,128)S(1)}, u32[]{:S(2)}, u32[]{:S(2)}) collective-permute-start(f32[4,256]{1,0:T(4,128)S(1)} %slice.132), channel_id=1, source_target_pairs={{0,4},{4,8},{8,12},{12,16},{16,20},{20,24},{24,28},{28,32},{32,36}... | collective-permute-start | bytes 12296 | tf_op jit(solution)/shard_map/ppermute | solution.py:15
  315.4 0.6 fusion.95
  316.0 0.1 collective-permute-done.1
  316.1 0.6 multiply_reduce_fusion.1
  316.7 246.6 %all-reduce = (f32[]{:T(128)}, f32[]{:T(128)}) all-reduce(f32[]{:T(128)} %multiply_reduce_fusion.1, f32[]{:T(128)} %fusion.95), channel_id=1, replica_groups=mesh['genome'=128,'rep'=4] {'genome'}, use_global_device_ids=true, to_apply=%region_5.6 | all-reduce | flops 2 | bytes 16 | tf_op jit(solution)/shard_map/psum | solution.py:80
  564.6 0.6 select_divide_fusion
  565.2 0.0 all-gather.5.cloned.1.call-update
  565.3 0.2 reduce-scatter.5.cloned.1.call-start
  565.5 0.9 fusion.46
  566.4 0.9 fusion.51
  567.3 76.0 %all-gather.5.cloned.1.call-done = f32[1024,256]{1,0:T(8,128)} async-done(((f32[8,256]{1,0:T(8,128)}), f32[1024,256]{1,0:T(8,128)}) %all-gather.5.cloned.1.call-update) | async-done | bytes 1048592 | tf_op jit(solution)/shard_map/all_gather | solution.py:65
  643.3 1.8 fusion.19
  645.1 2.1 fusion.17
  647.2 0.0 reduce-scatter.5.cloned.1.call-update
  647.2 2.2 collective-permute-start.2
  649.4 3.3 fusion
  652.7 0.6 gather_fusion.2
  653.3 4.1 fusion.2
  657.4 0.6 scatter_custom_fusion.2
  658.1 0.7 scatter_fusion.1
  658.7 1.4 fusion.53
  660.1 176.2 %reduce-scatter.5.cloned.1.call-done = f32[8,256]{1,0:T(8,128)} async-done(((f32[1024,256]{1,0:T(8,128)}), f32[8,256]{1,0:T(8,128)}) %reduce-scatter.5.cloned.1.call-update) | async-done | bytes 8208 | tf_op jit(solution)/shard_map/reduce_scatter | solution.py:75
  836.4 1.0 fusion.13
  837.3 13.0 %psum.41 = f32[12,256]{1,0:T(8,128)S(1)} all-reduce(f32[12,256]{1,0:T(8,128)S(1)} %fusion.13), channel_id=1, replica_groups=mesh['genome'=128,'rep'=4] {'rep'}, use_global_device_ids=true, to_apply=%region_11.12 | all-reduce | flops 3072 | bytes 24576 | tf_op jit(solution)/shard_map/psum | solution.py:77
  850.4 11.3 %collective-permute-start.3 = (f32[4,256]{1,0:T(4,128)S(1)}, f32[4,256]{1,0:T(4,128)S(1)}, u32[]{:S(2)}, u32[]{:S(2)}) collective-permute-start(f32[4,256]{1,0:T(4,128)S(1)} %slice.137), channel_id=1, source_target_pairs={{0,4},{4,8},{8,12},{12,16},{16,20},{20,24},{24,28},{28,32},{32,36}... | collective-permute-start | bytes 12296 | tf_op jit(solution)/shard_map/ppermute | solution.py:15
  861.7 0.7 collective-permute-done.3
  862.4 0.6 multiply_reduce_fusion
  863.0 246.6 %psum.42 = f32[]{:T(128)} all-reduce(f32[]{:T(128)} %multiply_reduce_fusion), channel_id=1, replica_groups=mesh['genome'=128,'rep'=4] {'genome'}, use_global_device_ids=true, to_apply=%region_13.14 | all-reduce | flops 1 | bytes 8 | tf_op jit(solution)/shard_map/psum | solution.py:80
  1110.9 0.6 copy.29
  1111.5 0.6 copy.30
  (42 shorter events, 0.2 us)
Async XLA Ops:
  7.2 14.0 %copy-start = (f32[6,256,256]{2,1,0:T(8,128)S(1)}, f32[6,256,256]{2,1,0:T(8,128)}, u32[]{:S(2)}) copy-start(f32[6,256,256]{2,1,0:T(8,128)} %param.15) | copy-start | bytes 4718596
  7.2 89.6 %all-gather.3.cloned.1.call-start = ((), (), s32[]{:S(2)}) async-start(), calls=%async_computation.2 | async-start | bytes 1056768 | tf_op jit(solution)/shard_map/all_gather | solution.py:65
  8.1 115.0 %collective-permute-start = (f32[4,256]{1,0:T(4,128)S(1)}, f32[4,256]{1,0:T(4,128)S(1)}, u32[]{:S(2)}, u32[]{:S(2)}) collective-permute-start(f32[4,256]{1,0:T(4,128)S(1)} %slice.111), channel_id=1, source_target_pairs={{4,0},{8,4},{12,8},{16,12},{20,16},{24,20},{28,24},{32,28},{36,32}... | collective-permute-start | bytes 12296 | tf_op jit(solution)/shard_map/ppermute | solution.py:15
  17.5 272.6 %reduce-scatter.3.cloned.1.call-start = ((), (), s32[]{:S(2)}) async-start(), calls=%async_computation.3 | async-start | bytes 1056768 | tf_op jit(solution)/shard_map/reduce_scatter | solution.py:75
  20.9 75.9 %copy-start.4 = (s32[6]{0:T(128)S(1)}, s32[6]{0:T(128)}, u32[]{:S(2)}) copy-start(s32[6]{0:T(128)} %param.17) | copy-start | bytes 76
  100.7 542.5 %all-gather.5.cloned.1.call-start = ((), (), s32[]{:S(2)}) async-start(), calls=%async_computation.4 | async-start | bytes 1056768 | tf_op jit(solution)/shard_map/all_gather | solution.py:65
  100.8 3.4 slice-start
  104.2 18.9 %copy-start.1 = (f32[8,256]{1,0:T(8,128)S(1)}, f32[8,256]{1,0:T(8,128)}, u32[]{:S(2)}) copy-start(f32[8,256]{1,0:T(8,128)} %reshape.239) | copy-start | bytes 24580
  127.9 187.5 %copy-start.3 = (s32[2048]{0:T(1024)S(1)}, s32[2048]{0:T(1024)}, u32[]{:S(2)}) copy-start(s32[2048]{0:T(1024)} %param.19) | copy-start | bytes 24580
  304.1 12.0 %collective-permute-start.1 = (f32[4,256]{1,0:T(4,128)S(1)}, f32[4,256]{1,0:T(4,128)S(1)}, u32[]{:S(2)}, u32[]{:S(2)}) collective-permute-start(f32[4,256]{1,0:T(4,128)S(1)} %slice.132), channel_id=1, source_target_pairs={{0,4},{4,8},{8,12},{12,16},{16,20},{20,24},{24,28},{28,32},{32,36}... | collective-permute-start | bytes 12296 | tf_op jit(solution)/shard_map/ppermute | solution.py:15
  565.3 271.1 %reduce-scatter.5.cloned.1.call-start = ((), (), s32[]{:S(2)}) async-start(), calls=%async_computation.5 | async-start | bytes 1056768 | tf_op jit(solution)/shard_map/reduce_scatter | solution.py:75
  567.3 79.9 %copy-start.2 = (f32[8,256]{1,0:T(8,128)S(1)}, f32[8,256]{1,0:T(8,128)}, u32[]{:S(2)}) copy-start(f32[8,256]{1,0:T(8,128)} %select_divide_fusion) | copy-start | bytes 24580
  647.2 5.5 collective-permute-start.2
  850.4 12.0 %collective-permute-start.3 = (f32[4,256]{1,0:T(4,128)S(1)}, f32[4,256]{1,0:T(4,128)S(1)}, u32[]{:S(2)}, u32[]{:S(2)}) collective-permute-start(f32[4,256]{1,0:T(4,128)S(1)} %slice.137), channel_id=1, source_target_pairs={{0,4},{4,8},{8,12},{12,16},{16,20},{20,24},{24,28},{28,32},{32,36}... | collective-permute-start | bytes 12296 | tf_op jit(solution)/shard_map/ppermute | solution.py:15
Sparse Core Ops, SparseCore 0:
  17.6 79.1 all-gather.2
  101.1 188.9 reduce-scatter.2
  565.4 77.8 all-gather.4
  647.4 188.8 reduce-scatter.4
where the time goes:
time: 1120 us
  blocking collectives  519 us (46%)
  waiting for transfers between devices  487 us (43%)
  starting transfers between devices  33.8 us (3%)
  matrix products  30.8 us (3%)
  local copies, waits for them, and re-layouts  22.8 us (2%)
  between operations  17.4 us (2%)
    psum x2, blocking collectives, shards(): lax.psum((jnp.sum(coverage * unmasked), jnp.sum(unmasked)), 'genome')  493 us
    reduce_scatter x2, waiting for transfers between devices, shards(): lax.psum_scatter(spread, 'genome', scatter_dimension=0, tiled=True)  336 us
    all_gather x2, waiting for transfers between devices, shards(): every_bias = lax.all_gather(weights, 'genome', axis=0, tiled=True)  151 us
    ppermute x4, starting transfers between devices, shifted(): return lax.ppermute(block, axis, route)  33.5 us
    psum x2, blocking collectives, shards(): summed = lax.psum(partial_value, 'rep')  26.1 us
  transfers between devices with their start and end apart: 8, of which 6 were waited for; matrix products, arithmetic and copies ran while one was open for 5% of the time, Pallas kernels for 0%

commit v1 on v0

v1 whole, which is shorter than its diff:
```python
import functools

import jax
import jax.numpy as jnp
from jax import lax
from jax.experimental import pallas as pl
from jax.experimental.pallas import tpu as pltpu
from jax.sharding import PartitionSpec as P

F32 = jnp.float32
I32 = jnp.int32
VMEM = pl.BlockSpec(memory_space=pltpu.VMEM)
SMEM = pl.BlockSpec(memory_space=pltpu.SMEM)
ROWS = 32
PARAMS = pltpu.CompilerParams(vmem_limit_bytes=32 * 1024 * 1024)


def rows_iota(shape):
    return lax.broadcasted_iota(I32, shape, 0)


def lanes_iota(shape):
    return lax.broadcasted_iota(I32, shape, 1)


def spread_blocks(flat):
    n = flat.shape[0] // 2
    halves = flat.reshape(n, 2, 128)
    return jnp.concatenate([halves[:, 0], halves[:, 1]], axis=1)


def columns_of(block_rows):
    width = block_rows.shape[1]
    padded = jnp.concatenate([block_rows, jnp.zeros((120, width), F32)], axis=0)
    return jnp.transpose(padded)


def pick_lane(ref, start, lane):
    chunk = ref[pl.ds(start, ROWS), :]
    hit = lanes_iota(chunk.shape) == lane
    return jnp.sum(jnp.where(hit, chunk, 0.0), axis=1, keepdims=True)


def fold(chunk):
    total = chunk[0:8]
    for at in range(8, chunk.shape[0], 8):
        total = total + chunk[at : at + 8]
    return total


def request_kernel(masked_ref, cols_ref, count_ref, code_ref, own_ref, ahead_ref, *, blk_g):
    groups, lanes = code_ref.shape
    row = rows_iota((groups, lanes))
    code = jnp.zeros((groups, lanes), I32)
    for t in range(cols_ref.shape[0]):
        target = cols_ref[t] // blk_g
        wanted = cols_ref[t] - target * blk_g + 1
        used = t < count_ref[0]
        code = jnp.where((row == target) & used, wanted, code)
    code_ref[...] = code
    for c in range(blk_g):
        for h in range(2):
            piece = 1.0 - masked_ref[pl.ds(2 * c + h, 1), :].astype(F32)
            own_ref[pl.ds(c, 1), pl.ds(128 * h, 128)] = piece
            if c < ahead_ref.shape[0]:
                ahead_ref[pl.ds(c, 1), pl.ds(128 * h, 128)] = piece


def band_columns(band_ref, cols_scr, out_scr, anchor):
    blk_dev, spans, width, _ = band_ref.shape
    for q in range(blk_dev):
        def step(s, sums, q=q):
            start = pl.multiple_of(s * ROWS, ROWS)
            here = pick_lane(cols_scr, start, anchor + q)
            out = []
            for k in range(spans):
                chunk = band_ref[q, k, pl.ds(start, ROWS), :]
                if k == 0:
                    above = rows_iota(chunk.shape) + start < lanes_iota(chunk.shape)
                    chunk = jnp.where(above, chunk, 0.0)
                out.append(sums[k] + fold(chunk * here))
            return tuple(out)

        sums = lax.fori_loop(
            0, width // ROWS, step, tuple(jnp.zeros((8, width), F32) for _ in range(spans))
        )
        for k in range(spans):
            out_scr[pl.ds(anchor + q + k, 1), :] += jnp.sum(sums[k], axis=0, keepdims=True)


def band_rows(band_ref, ext_scr, racc_scr, anchor):
    blk_dev, spans, width, _ = band_ref.shape
    for q in range(blk_dev):
        biases = [ext_scr[pl.ds(anchor + q + k, 1), :] for k in range(spans)]

        def step(s, carry, q=q, biases=biases):
            start = pl.multiple_of(s * ROWS, ROWS)
            total = jnp.zeros((ROWS, width), F32)
            for k in range(spans):
                chunk = band_ref[q, k, pl.ds(start, ROWS), :]
                if k == 0:
                    upper = rows_iota(chunk.shape) + start <= lanes_iota(chunk.shape)
                    chunk = jnp.where(upper, chunk, 0.0)
                total = total + chunk * biases[k]
            summed = jnp.sum(total, axis=1, keepdims=True)
            hit = lanes_iota((ROWS, 128)) == anchor + q
            racc_scr[pl.ds(start, ROWS), :] += jnp.where(hit, summed, 0.0)
            return carry

        lax.fori_loop(0, width // ROWS, step, 0)


def trans_columns(trans_ref, rows_ref, count_ref, cols_scr, base, y_ref):
    tiles, width, _ = trans_ref.shape
    y_ref[...] = jnp.zeros(y_ref.shape, F32)

    def one(t, carry):
        lane = jnp.where(t < count_ref[0], rows_ref[t] - base, 127)

        def step(s, total):
            start = pl.multiple_of(s * ROWS, ROWS)
            here = pick_lane(cols_scr, start, lane)
            return total + fold(trans_ref[t, pl.ds(start, ROWS), :] * here)

        total = lax.fori_loop(0, width // ROWS, step, jnp.zeros((8, width), F32), unroll=True)
        y_ref[pl.ds(t, 1), :] = jnp.sum(total, axis=0, keepdims=True)
        return carry

    lax.fori_loop(0, tiles, one, 0)


def trans_rows_sum(trans_ref, rows_ref, cols_ref, count_ref, got_ref, racc_scr, base, blk_g):
    tiles, width, _ = trans_ref.shape

    def one(t, carry):
        used = t < count_ref[0]
        lane = jnp.where(used, rows_ref[t] - base, 127)
        source = jnp.where(used, cols_ref[t] // blk_g, 0)
        bias = got_ref[pl.ds(source, 1), :]

        def step(s, c):
            start = pl.multiple_of(s * ROWS, ROWS)
            summed = jnp.sum(trans_ref[t, pl.ds(start, ROWS), :] * bias, axis=1, keepdims=True)
            hit = lanes_iota((ROWS, 128)) == lane
            racc_scr[pl.ds(start, ROWS), :] += jnp.where(hit, summed, 0.0)
            return c

        lax.fori_loop(0, width // ROWS, step, 0, unroll=True)
        return carry

    lax.fori_loop(0, tiles, one, 0)


def owner_sums(code_ref, got_ref, blk_g):
    width = got_ref.shape[1]
    out = []
    for c in range(blk_g):
        total = jnp.zeros((8, width), F32)
        for at in range(0, code_ref.shape[0], 8):
            hit = code_ref[at : at + 8, :] == c + 1
            hit = jnp.concatenate([hit] * (width // 128), axis=1)
            total = total + jnp.where(hit, got_ref[at : at + 8, :], 0.0)
        out.append(jnp.sum(total, axis=0, keepdims=True))
    return jnp.concatenate(out, axis=0)


def pack(code_ref, own, y_ref, cols_ref, count_ref, send_ref, blk_g):
    groups, width = send_ref.shape
    for at in range(0, groups, 8):
        code = code_ref[at : at + 8, :]
        for h in range(0, width, 128):
            piece = jnp.zeros((8, 128), F32)
            for c in range(blk_g):
                piece = jnp.where(code == c + 1, own[c : c + 1, h : h + 128], piece)
            send_ref[at : at + 8, h : h + 128] = piece
    for t in range(cols_ref.shape[0]):
        @pl.when(t < count_ref[0])
        def _(t=t):
            send_ref[pl.ds(cols_ref[t] // blk_g, 1), :] = y_ref[pl.ds(t, 1), :]


def first_kernel(own_ref, ahead_ref, band_ref, trans_ref, rows_ref, count_ref,
                 y_ref, part_ref, spill_ref, ext_scr, cols_scr, racc_scr, csum_scr):
    blk_g = own_ref.shape[0]
    reach = ahead_ref.shape[0]
    anchor = lax.axis_index("rep") * band_ref.shape[0]
    base = lax.axis_index("genome") * blk_g
    own = own_ref[...]
    ext_scr[0:blk_g, :] = own
    ext_scr[blk_g : blk_g + reach, :] = ahead_ref[...]
    cols_scr[...] = columns_of(own)
    racc_scr[...] = jnp.zeros(racc_scr.shape, F32)
    csum_scr[...] = jnp.zeros(csum_scr.shape, F32)
    trans_columns(trans_ref, rows_ref, count_ref, cols_scr, base, y_ref)
    band_columns(band_ref, cols_scr, csum_scr, anchor)
    band_rows(band_ref, ext_scr, racc_scr, anchor)
    part_ref[...] = csum_scr[0:blk_g, :] + jnp.transpose(racc_scr[...])[0:blk_g, :]
    spill_ref[...] = csum_scr[blk_g : blk_g + reach, :]


def pack_kernel(code_ref, own_ref, y_ref, cols_ref, count_ref, send_ref):
    pack(code_ref, own_ref[...], y_ref, cols_ref, count_ref, send_ref, own_ref.shape[0])


def gather_kernel(code_ref, got_ref, part_ref, back_ref, trans_ref, rows_ref, cols_ref, count_ref,
                  share_ref, racc_scr):
    blk_g, width = part_ref.shape
    reach = back_ref.shape[0]
    base = lax.axis_index("genome") * blk_g
    racc_scr[...] = jnp.zeros(racc_scr.shape, F32)
    trans_rows_sum(trans_ref, rows_ref, cols_ref, count_ref, got_ref, racc_scr, base, blk_g)
    total = part_ref[...] + jnp.transpose(racc_scr[...])[0:blk_g, :]
    total = total + owner_sums(code_ref, got_ref, blk_g)
    total = total + jnp.concatenate([back_ref[...], jnp.zeros((blk_g - reach, width), F32)], axis=0)
    for s in range(share_ref.shape[0]):
        share_ref[s] = total


def second_kernel(shares_ref, own_ref, code_ref, band_ref, trans_ref, rows_ref, cols_ref, count_ref,
                  bias_ref, send_ref, ahead_ref, spill_ref, part_ref, first_ref,
                  cols_scr, csum_scr, y_scr):
    blk_g = own_ref.shape[0]
    reach = ahead_ref.shape[0]
    anchor = lax.axis_index("rep") * band_ref.shape[0]
    base = lax.axis_index("genome") * blk_g
    own = own_ref[...]
    total = shares_ref[0]
    for s in range(1, shares_ref.shape[0]):
        total = total + shares_ref[s]
    kept = own > 0.0
    bias = jnp.where(kept, 1.0 / jnp.where(kept, total, 1.0), 0.0)
    bias_ref[...] = bias
    ahead_ref[...] = bias[0:reach]
    first_ref[...] = jnp.where(kept, total, 0.0)
    cols_scr[...] = columns_of(bias)
    csum_scr[...] = jnp.zeros(csum_scr.shape, F32)
    trans_columns(trans_ref, rows_ref, count_ref, cols_scr, base, y_scr)
    band_columns(band_ref, cols_scr, csum_scr, anchor)
    part_ref[...] = csum_scr[0:blk_g, :]
    spill_ref[...] = csum_scr[blk_g : blk_g + reach, :]
    pack(code_ref, bias, y_scr, cols_ref, count_ref, send_ref, blk_g)


def third_kernel(code_ref, got_ref, part_ref, back_ref, bias_ref, ahead_ref, band_ref, trans_ref,
                 rows_ref, cols_ref, count_ref, share_ref, ext_scr, racc_scr):
    blk_g, width = part_ref.shape
    reach = back_ref.shape[0]
    anchor = lax.axis_index("rep") * band_ref.shape[0]
    base = lax.axis_index("genome") * blk_g
    ext_scr[0:blk_g, :] = bias_ref[...]
    ext_scr[blk_g : blk_g + reach, :] = ahead_ref[...]
    racc_scr[...] = jnp.zeros(racc_scr.shape, F32)
    band_rows(band_ref, ext_scr, racc_scr, anchor)
    trans_rows_sum(trans_ref, rows_ref, cols_ref, count_ref, got_ref, racc_scr, base, blk_g)
    total = part_ref[...] + jnp.transpose(racc_scr[...])[0:blk_g, :]
    total = total + owner_sums(code_ref, got_ref, blk_g)
    total = total + jnp.concatenate([back_ref[...], jnp.zeros((blk_g - reach, width), F32)], axis=0)
    for s in range(share_ref.shape[0]):
        share_ref[s] = total


def whole_sum(block):
    return jnp.sum(jnp.sum(block, axis=0, keepdims=True), axis=1, keepdims=True)


def stats_kernel(shares_ref, own_ref, bias_ref, first_ref, second_ref, stats_ref):
    total = shares_ref[0]
    for s in range(1, shares_ref.shape[0]):
        total = total + shares_ref[s]
    second_ref[...] = total
    count = whole_sum(own_ref[...])
    sum_one = whole_sum(first_ref[...])
    scale = sum_one / jnp.maximum(count, 1.0)
    scale = jnp.where(scale == 0.0, 1.0, scale)
    sum_two = whole_sum((bias_ref[...] * scale) * (total * scale))
    lane = lanes_iota(stats_ref.shape)
    stats = jnp.where(lane == 0, sum_one, 0.0)
    stats = jnp.where(lane == 1, sum_two, stats)
    stats = jnp.where(lane == 2, scale, stats)
    stats_ref[...] = jnp.where(lane == 3, count, stats)


def final_kernel(stats_ref, own_ref, bias_ref, second_ref, weights_ref, coverage_ref):
    stats = stats_ref[...]
    lane = lanes_iota(stats.shape)

    def lane_of(at):
        return jnp.sum(jnp.where(lane == at, stats, 0.0), axis=1, keepdims=True)

    count = jnp.sum(lane_of(3), axis=0, keepdims=True)
    average_one = jnp.sum(lane_of(0), axis=0, keepdims=True) / count
    ratio = average_one / lane_of(2)
    average_two = jnp.sum(lane_of(1) * ratio * ratio, axis=0, keepdims=True) / count
    own = own_ref[...]
    kept = own > 0.0
    total = second_ref[...] * average_one
    coverage = (bias_ref[...] * average_one) * total
    weights = jnp.where(kept, average_two / jnp.where(kept, total, 1.0), 0.0)
    for c in range(own.shape[0]):
        for h in range(2):
            weights_ref[pl.ds(2 * c + h, 1), :] = weights[c : c + 1, 128 * h : 128 * h + 128]
            coverage_ref[pl.ds(2 * c + h, 1), :] = coverage[c : c + 1, 128 * h : 128 * h + 128]


def call(kernel, outs, specs, scratch=()):
    return pl.pallas_call(
        kernel,
        out_shape=[jax.ShapeDtypeStruct(s, d) for s, d in outs],
        in_specs=list(specs),
        out_specs=[VMEM] * len(outs),
        scratch_shapes=[pltpu.VMEM(s, F32) for s in scratch],
        compiler_params=PARAMS,
    )


def shifted(block, axis, distance):
    devices = range(lax.axis_size(axis))
    route = [(i - distance, i) for i in devices if i - distance in devices]
    return lax.ppermute(block, axis, route)


def exchange(block, axis):
    return lax.all_to_all(block, axis, 0, 0, tiled=True)


def shards(band_tiles, trans_tiles, trans_rows, trans_cols, trans_count, masked):
    blk_dev, spans, width, _ = band_tiles.shape
    reach = spans - 1
    replicas = lax.axis_size("rep")
    groups = lax.axis_size("genome")
    blk_g = blk_dev * replicas
    halves = masked.reshape(2 * blk_g, 128)
    own_shape = (blk_g, width)
    reach_shape = (reach, width)
    code, own, ahead = call(
        functools.partial(request_kernel, blk_g=blk_g),
        [((groups, 128), I32), (own_shape, F32), (reach_shape, F32)],
        [VMEM, SMEM, SMEM],
    )(halves, trans_cols, trans_count)
    forward = shifted(ahead, "genome", -1)
    code = exchange(code, "genome")
    y, part, spill = call(
        first_kernel,
        [((8, width), F32), (own_shape, F32), (reach_shape, F32)],
        [VMEM] * 4 + [SMEM] * 2,
        [(16, width), (width, 128), (width, 128), (16, width)],
    )(own, forward, band_tiles, trans_tiles, trans_rows, trans_count)
    back = shifted(spill, "genome", 1)
    (send,) = call(
        pack_kernel, [((groups, width), F32)], [VMEM] * 3 + [SMEM] * 2
    )(code, own, y, trans_cols, trans_count)
    got = exchange(send, "genome")
    (share,) = call(
        gather_kernel,
        [((replicas,) + own_shape, F32)],
        [VMEM] * 5 + [SMEM] * 3,
        [(width, 128)],
    )(code, got, part, back, trans_tiles, trans_rows, trans_cols, trans_count)
    shares = exchange(share, "rep")
    bias, send, ahead, spill, part, first = call(
        second_kernel,
        [(own_shape, F32), ((groups, width), F32), (reach_shape, F32), (reach_shape, F32),
         (own_shape, F32), (own_shape, F32)],
        [VMEM] * 5 + [SMEM] * 3,
        [(width, 128), (16, width), (8, width)],
    )(shares, own, code, band_tiles, trans_tiles, trans_rows, trans_cols, trans_count)
    forward = shifted(ahead, "genome", -1)
    back = shifted(spill, "genome", 1)
    got = exchange(send, "genome")
    (share,) = call(
        third_kernel,
        [((replicas,) + own_shape, F32)],
        [VMEM] * 8 + [SMEM] * 3,
        [(16, width), (width, 128)],
    )(code, got, part, back, bias, forward, band_tiles, trans_tiles, trans_rows, trans_cols,
      trans_count)
    shares = exchange(share, "rep")
    second, stats = call(
        stats_kernel, [(own_shape, F32), ((groups, 128), F32)], [VMEM] * 4
    )(shares, own, bias, first)
    stats = exchange(stats, "genome")
    weights, coverage = call(
        final_kernel, [((2 * blk_g, 128), F32)] * 2, [VMEM] * 4
    )(stats, own, bias, second)
    return (weights.reshape(-1), coverage.reshape(-1))


def solution(mesh):
    in_specs = (
        P(("genome", "rep"), None, None, None),
        P(("genome", "rep"), None, None),
        P(("genome", "rep")),
        P(("genome", "rep")),
        P(("genome", "rep")),
        P("genome"),
    )
    out_specs = (P("genome"), P("genome"))
    return jax.shard_map(shards, mesh=mesh, in_specs=in_specs, out_specs=out_specs, check_vma=False)
```

time: 1120 us -> 134 us (0.12)
  blocking collectives: 519 us -> 36.8 us
  waiting for transfers between devices: 487 us -> 17.8 us
  matrix products: 30.8 us -> 0 us
  starting transfers between devices: 33.8 us -> 52.4 us
  between operations: 17.4 us -> 1.46 us
  Pallas kernels: 0 us -> 14.7 us
  local copies, waits for them, and re-layouts: 22.8 us -> 10.2 us
    psum x4 -> x0, blocking collectives: 519 us -> none  [the longest x2 493 us: shards(): lax.psum((jnp.sum(coverage * unmasked), jnp.sum(unmasked)), 'genome')]
    reduce_scatter x2 -> x0, waiting for transfers between devices: 336 us -> none  [shards(): lax.psum_scatter(spread, 'genome', scatter_dimension=0, tiled=True)]
    all_gather x2 -> x0, waiting for transfers between devices: 151 us -> none  [shards(): every_bias = lax.all_gather(weights, 'genome', axis=0, tiled=True)]
    all_to_all x0 -> x3, starting transfers between devices: none -> 40.6 us  [exchange(): return lax.all_to_all(block, axis, 0, 0, tiled=True)]
    all_to_all x0 -> x3, blocking collectives: none -> 36.8 us  [exchange(): return lax.all_to_all(block, axis, 0, 0, tiled=True)]
    dot_general x16 -> x0, matrix products: 30.8 us -> none  [the longest x2 8.22 us: shards(): jnp.einsum('qkij,qkj->qi', masked_tiles, column_bias, precision=HIGH)]
    ppermute x4, starting transfers between devices: 33.5 us -> 11.8 us  [shifted(): return lax.ppermute(block, axis, route)]
    all_to_all x0 -> x3, waiting for transfers between devices: none -> 15.4 us  [exchange(): return lax.all_to_all(block, axis, 0, 0, tiled=True)]
  transfers between devices with their start and end apart: 8 -> 7, of which waited for: 6 -> 3; matrix products, arithmetic and copies ran while one was open for 5% -> 0% of each run, Pallas kernels for 0% -> 3%
where the time goes in v1:
time: 134 us; the launch traced here: 133 us
  starting transfers between devices  52.4 us (39%)
  blocking collectives  36.8 us (27%)
  waiting for transfers between devices  17.8 us (13%)
  Pallas kernels  14.7 us (11%)
  local copies, waits for them, and re-layouts  10.2 us (8%)
  between operations  1.46 us (1%)
    all_to_all x3, starting transfers between devices, exchange(): return lax.all_to_all(block, axis, 0, 0, tiled=True)  40.6 us
    all_to_all x3, blocking collectives, exchange(): return lax.all_to_all(block, axis, 0, 0, tiled=True)  36.8 us
    all_to_all x3, waiting for transfers between devices, exchange(): return lax.all_to_all(block, axis, 0, 0, tiled=True)  15.4 us
    ppermute x4, starting transfers between devices, shifted(): return lax.ppermute(block, axis, route)  11.8 us
    unnamed x22, local copies, waits for them, and re-layouts  8.66 us
    pallas_call x1, Pallas kernels, shards(): call(first_kernel, [((8, width), F32), (own_shape, F32), (reach_shape, F3...  4.52 us
    pallas_call x1, Pallas kernels, shards(): call(second_kernel, [(own_shape, F32), ((groups, width), F32), (reach_sha...  3.06 us
    pallas_call x1, Pallas kernels, shards(): call(third_kernel, [((replicas,) + own_shape, F32)], [VMEM] * 8 + [SMEM]...  2.91 us
  transfers between devices with their start and end apart: 7, of which 3 were waited for; matrix products, arithmetic and copies ran while one was open for 0% of the time, Pallas kernels for 3%

profile of v1, /device:TPU:1, one launch (start us, length us, event | category | flops | bytes accessed | tf_op | source)
XLA Modules:
  0.0 133.5 jit_solution(6810249885594801085)
XLA Ops:
  0.6 0.0 copy-start.6
  1.3 0.0 copy-start.5
  1.3 0.6 copy-done.5
  2.0 0.0 copy-start.7
  2.0 0.7 copy-done.7
  2.7 1.2 shard_map.77
  3.9 18.4 %all-to-all-start = ((s32[128,1,128]{2,1,0:T(1,128)}), s32[128,1,128]{2,1,0:T(1,128)S(1)}, u32[]{:S(2)}, u32[]{:S(2)}) async-start(s32[128,1,128]{2,1,0:T(1,128)} %bitcast.2), calls=%async_computation | async-start | bytes 131072 | tf_op jit(solution)/shard_map/all_to_all | solution.py:323
  22.3 0.0 copy-start.9
  22.3 2.8 %collective-permute-start = (f32[4,256]{1,0:T(4,128)S(1)}, f32[4,256]{1,0:T(4,128)S(1)}, u32[]{:S(2)}, u32[]{:S(2)}) collective-permute-start(f32[4,256]{1,0:T(4,128)S(1)} %get-tuple-element.20), channel_id=1, source_target_pairs={{4,0},{8,4},{12,8},{16,12},{20,16},{24,20},{28,24},{32,28},{36,32}... | collective-permute-start | bytes 12296 | tf_op jit(solution)/shard_map/ppermute | solution.py:319
  25.1 2.4 %collective-permute-done.ahead_ref = f32[4,256]{1,0:T(4,128)S(1)} collective-permute-done((f32[4,256]{1,0:T(4,128)S(1)}, f32[4,256]{1,0:T(4,128)S(1)}, u32[]{:S(2)}, u32[]{:S(2)}) %collective-permute-start) | collective-permute-done | bytes 4128 | tf_op jit(solution)/shard_map/ppermute | solution.py:319
  27.5 0.0 copy-start
  27.6 1.4 %copy-done = f32[6,256,256]{2,1,0:T(8,128)S(1)} copy-done((f32[6,256,256]{2,1,0:T(8,128)S(1)}, f32[6,256,256]{2,1,0:T(8,128)}, u32[]{:S(2)}) %copy-start) | copy-done | bytes 1572888
  29.0 0.0 copy-start.2
  29.0 1.7 %copy-done.2 = f32[2,5,256,256]{3,2,1,0:T(8,128)S(1)} copy-done((f32[2,5,256,256]{3,2,1,0:T(8,128)S(1)}, f32[2,5,256,256]{3,2,1,0:T(8,128)}, u32[]{:S(2)}) %copy-start.2) | copy-done | bytes 2621464
  30.7 0.0 copy-start.8
  30.7 0.7 copy-done.8
  31.4 0.0 copy-start.1
  31.4 4.5 %shard_map.78 = (f32[8,256]{1,0:T(8,128)S(1)}, f32[8,256]{1,0:T(8,128)S(1)}, f32[4,256]{1,0:T(4,128)S(1)}) custom-call(f32[8,256]{1,0:T(8,128)S(1)} %get-tuple-element.19.own_ref, f32[4,256]{1,0:T(4,128)S(1)} %collective-permute-done.ahead_ref, f32[2,5,256,256]{3,2,1,0:T(8,128)S(1)} %copy-done.2, f32[6,256,256]{2,1,0:T(8,128)S(1)} %copy-done, ...), custom_call_target="tpu_custom_call" | custom-call | tf_op jit(solution)/shard_map/pallas_call | solution.py:342
  35.9 0.0 all-to-all-done
  35.9 0.0 copy-done.6
  35.9 0.7 shard_map.79
  36.6 0.8 copy.9
  37.4 13.2 %all-to-all-start.1 = ((f32[128,1,256]{2,1,0:T(1,128)}), f32[128,1,256]{2,1,0:T(1,128)S(1)}, u32[]{:S(2)}, u32[]{:S(2)}) async-start(f32[128,1,256]{2,1,0:T(1,128)} %copy.9), calls=%async_computation.1 | async-start | bytes 262144 | tf_op jit(solution)/shard_map/all_to_all | solution.py:323
  50.5 3.5 %collective-permute-start.1 = (f32[4,256]{1,0:T(4,128)S(1)}, f32[4,256]{1,0:T(4,128)S(1)}, u32[]{:S(2)}, u32[]{:S(2)}) collective-permute-start(f32[4,256]{1,0:T(4,128)S(1)} %get-tuple-element.23), channel_id=1, source_target_pairs={{0,4},{4,8},{8,12},{12,16},{16,20},{20,24},{24,28},{28,32},{32,36}... | collective-permute-start | bytes 12296 | tf_op jit(solution)/shard_map/ppermute | solution.py:319
  54.1 8.7 %all-to-all-done.1 = f32[128,1,256]{2,1,0:T(1,128)S(1)} async-done(((f32[128,1,256]{2,1,0:T(1,128)}), f32[128,1,256]{2,1,0:T(1,128)S(1)}, u32[]{:S(2)}, u32[]{:S(2)}) %all-to-all-start.1) | async-done | bytes 131104 | tf_op jit(solution)/shard_map/all_to_all | solution.py:323
  62.8 0.0 collective-permute-done.1.back_ref
  62.8 0.0 copy-done.9
  62.8 0.0 copy-done.1
  62.8 1.4 %shard_map.80 = f32[4,8,256]{2,1,0:T(8,128)S(1)} custom-call(s32[128,128]{1,0:T(8,128)S(1)} %bitcast.20, f32[128,256]{1,0:T(8,128)S(1)} %bitcast.24, f32[8,256]{1,0:T(8,128)S(1)} %get-tuple-element.22.part_ref, f32[4,256]{1,0:T(4,128)S(1)} %collective-permute-done.1.back_ref, f32[6,256,256]{2,1,0:T(8,128)S(1)} %copy-done.1, s32[6]{0:T(128)S(1)} %copy-done.9, ...), custom_call_target="tpu_custom_call" | custom-call | tf_op jit(solution)/shard_map/pallas_call | solution.py:353
  64.2 8.1 %all_to_all.54.shares_ref = f32[4,8,256]{2,1,0:T(8,128)S(1)} all-to-all(f32[4,8,256]{2,1,0:T(8,128)S(1)} %shard_map.80), channel_id=1, replica_groups=mesh['genome'=128,'rep'=4] {'rep'}, dimensions={0} | all-to-all | bytes 65536 | tf_op jit(solution)/shard_map/all_to_all | solution.py:323
  72.3 0.0 copy-start.3
  72.3 1.7 %copy-done.3 = f32[2,5,256,256]{3,2,1,0:T(8,128)S(1)} copy-done((f32[2,5,256,256]{3,2,1,0:T(8,128)S(1)}, f32[2,5,256,256]{3,2,1,0:T(8,128)}, u32[]{:S(2)}) %copy-start.3) | copy-done | bytes 2621464
  74.0 3.1 %shard_map.81 = (f32[8,256]{1,0:T(8,128)S(1)}, f32[128,256]{1,0:T(8,128)S(1)}, f32[4,256]{1,0:T(4,128)S(1)}, f32[4,256]{1,0:T(4,128)S(1)}, f32[8,256]{1,0:T(8,128)S(1)}, /*index=5*/f32[8,256]{1,0:T(8,128)S(1)}) custom-call(f32[4,8,256]{2,1,0:T(8,128)S(1)} %all_to_all.54.shares_ref, f32[8,256]{1,0:T(8,128)S(1)} %get-tuple-element.19.own_ref, ...), custom_call_target="tpu_custom_call" | custom-call | tf_op jit(solution)/shard_map/pallas_call | solution.py:360
  77.1 0.8 copy.10
  77.9 9.0 %all-to-all-start.3 = ((f32[128,1,256]{2,1,0:T(1,128)}), f32[128,1,256]{2,1,0:T(1,128)S(1)}, u32[]{:S(2)}, u32[]{:S(2)}) async-start(f32[128,1,256]{2,1,0:T(1,128)} %copy.10), calls=%async_computation.3 | async-start | bytes 262144 | tf_op jit(solution)/shard_map/all_to_all | solution.py:323
  86.9 3.5 %collective-permute-start.2 = (f32[4,256]{1,0:T(4,128)S(1)}, f32[4,256]{1,0:T(4,128)S(1)}, u32[]{:S(2)}, u32[]{:S(2)}) collective-permute-start(f32[4,256]{1,0:T(4,128)S(1)} %get-tuple-element.26), channel_id=1, source_target_pairs={{0,4},{4,8},{8,12},{12,16},{16,20},{20,24},{24,28},{28,32},{32,36}... | collective-permute-start | bytes 12296 | tf_op jit(solution)/shard_map/ppermute | solution.py:319
  90.5 1.9 %collective-permute-start.3 = (f32[4,256]{1,0:T(4,128)S(1)}, f32[4,256]{1,0:T(4,128)S(1)}, u32[]{:S(2)}, u32[]{:S(2)}) collective-permute-start(f32[4,256]{1,0:T(4,128)S(1)} %get-tuple-element.28), channel_id=1, source_target_pairs={{4,0},{8,4},{12,8},{16,12},{20,16},{24,20},{28,24},{32,28},{36,32}... | collective-permute-start | bytes 12296 | tf_op jit(solution)/shard_map/ppermute | solution.py:319
  92.4 6.7 %all-to-all-done.3 = f32[128,1,256]{2,1,0:T(1,128)S(1)} async-done(((f32[128,1,256]{2,1,0:T(1,128)}), f32[128,1,256]{2,1,0:T(1,128)S(1)}, u32[]{:S(2)}, u32[]{:S(2)}) %all-to-all-start.3) | async-done | bytes 131104 | tf_op jit(solution)/shard_map/all_to_all | solution.py:323
  99.1 0.0 collective-permute-done.2.back_ref
  99.2 0.0 collective-permute-done.3.ahead_ref
  99.2 0.0 copy-start.4
  99.2 1.7 %copy-done.4 = f32[2,5,256,256]{3,2,1,0:T(8,128)S(1)} copy-done((f32[2,5,256,256]{3,2,1,0:T(8,128)S(1)}, f32[2,5,256,256]{3,2,1,0:T(8,128)}, u32[]{:S(2)}) %copy-start.4) | copy-done | bytes 2621464
  100.9 2.9 %shard_map.82 = f32[4,8,256]{2,1,0:T(8,128)S(1)} custom-call(s32[128,128]{1,0:T(8,128)S(1)} %bitcast.22, f32[128,256]{1,0:T(8,128)S(1)} %bitcast.25, f32[8,256]{1,0:T(8,128)S(1)} %get-tuple-element.25.part_ref, f32[4,256]{1,0:T(4,128)S(1)} %collective-permute-done.2.back_ref, f32[8,256]{1,0:T(8,128)S(1)} %get-tuple-element.27.bias_ref, ...), custom_call_target="tpu_custom_call" | custom-call | tf_op jit(solution)/shard_map/pallas_call | solution.py:370
  103.8 6.7 %all_to_all.55.shares_ref = f32[4,8,256]{2,1,0:T(8,128)S(1)} all-to-all(f32[4,8,256]{2,1,0:T(8,128)S(1)} %shard_map.82), channel_id=1, replica_groups=mesh['genome'=128,'rep'=4] {'rep'}, dimensions={0} | all-to-all | bytes 65536 | tf_op jit(solution)/shard_map/all_to_all | solution.py:323
  110.5 0.2 shard_map.83
  110.7 22.1 %all_to_all.56 = f32[128,1,128]{2,1,0:T(1,128)S(1)} all-to-all(f32[128,1,128]{2,1,0:T(1,128)S(1)} %bitcast.28), channel_id=1, replica_groups=mesh['genome'=128,'rep'=4] {'genome'}, dimensions={0} | all-to-all | bytes 131072 | tf_op jit(solution)/shard_map/all_to_all | solution.py:323
  132.7 0.8 shard_map.84
  (2 shorter events, 0.0 us)
Async XLA Ops:
  0.6 35.3 %copy-start.6 = (s32[6]{0:T(128)S(1)}, s32[6]{0:T(128)}, u32[]{:S(2)}) copy-start(s32[6]{0:T(128)} %cols_ref.9) | copy-start | bytes 76
  1.3 0.7 copy-start.5
  2.0 0.7 copy-start.7
  3.9 32.0 %all-to-all-start = ((s32[128,1,128]{2,1,0:T(1,128)}), s32[128,1,128]{2,1,0:T(1,128)S(1)}, u32[]{:S(2)}, u32[]{:S(2)}) async-start(s32[128,1,128]{2,1,0:T(1,128)} %bitcast.2), calls=%async_computation | async-start | bytes 131072 | tf_op jit(solution)/shard_map/all_to_all | solution.py:323
  22.3 40.5 %copy-start.9 = (s32[6]{0:T(128)S(1)}, s32[6]{0:T(128)}, u32[]{:S(2)}) copy-start(s32[6]{0:T(128)} %rows_ref.7) | copy-start | bytes 76
  22.3 5.2 %collective-permute-start = (f32[4,256]{1,0:T(4,128)S(1)}, f32[4,256]{1,0:T(4,128)S(1)}, u32[]{:S(2)}, u32[]{:S(2)}) collective-permute-start(f32[4,256]{1,0:T(4,128)S(1)} %get-tuple-element.20), channel_id=1, source_target_pairs={{4,0},{8,4},{12,8},{16,12},{20,16},{24,20},{28,24},{32,28},{36,32}... | collective-permute-start | bytes 12296 | tf_op jit(solution)/shard_map/ppermute | solution.py:319
  27.5 1.4 %copy-start = (f32[6,256,256]{2,1,0:T(8,128)S(1)}, f32[6,256,256]{2,1,0:T(8,128)}, u32[]{:S(2)}) copy-start(f32[6,256,256]{2,1,0:T(8,128)} %trans_ref.7) | copy-start | bytes 4718596
  29.0 1.7 %copy-start.2 = (f32[2,5,256,256]{3,2,1,0:T(8,128)S(1)}, f32[2,5,256,256]{3,2,1,0:T(8,128)}, u32[]{:S(2)}) copy-start(f32[2,5,256,256]{3,2,1,0:T(8,128)} %band_ref.5) | copy-start | bytes 7864324
  30.7 0.7 copy-start.8
  31.4 31.4 %copy-start.1 = (f32[6,256,256]{2,1,0:T(8,128)S(1)}, f32[6,256,256]{2,1,0:T(8,128)}, u32[]{:S(2)}) copy-start(f32[6,256,256]{2,1,0:T(8,128)} %trans_ref.7) | copy-start | bytes 4718596
  37.4 25.4 %all-to-all-start.1 = ((f32[128,1,256]{2,1,0:T(1,128)}), f32[128,1,256]{2,1,0:T(1,128)S(1)}, u32[]{:S(2)}, u32[]{:S(2)}) async-start(f32[128,1,256]{2,1,0:T(1,128)} %copy.9), calls=%async_computation.1 | async-start | bytes 262144 | tf_op jit(solution)/shard_map/all_to_all | solution.py:323
  50.5 12.2 %collective-permute-start.1 = (f32[4,256]{1,0:T(4,128)S(1)}, f32[4,256]{1,0:T(4,128)S(1)}, u32[]{:S(2)}, u32[]{:S(2)}) collective-permute-start(f32[4,256]{1,0:T(4,128)S(1)} %get-tuple-element.23), channel_id=1, source_target_pairs={{0,4},{4,8},{8,12},{12,16},{16,20},{20,24},{24,28},{28,32},{32,36}... | collective-permute-start | bytes 12296 | tf_op jit(solution)/shard_map/ppermute | solution.py:319
  72.3 1.7 %copy-start.3 = (f32[2,5,256,256]{3,2,1,0:T(8,128)S(1)}, f32[2,5,256,256]{3,2,1,0:T(8,128)}, u32[]{:S(2)}) copy-start(f32[2,5,256,256]{3,2,1,0:T(8,128)} %band_ref.5) | copy-start | bytes 7864324
  77.9 21.3 %all-to-all-start.3 = ((f32[128,1,256]{2,1,0:T(1,128)}), f32[128,1,256]{2,1,0:T(1,128)S(1)}, u32[]{:S(2)}, u32[]{:S(2)}) async-start(f32[128,1,256]{2,1,0:T(1,128)} %copy.10), calls=%async_computation.3 | async-start | bytes 262144 | tf_op jit(solution)/shard_map/all_to_all | solution.py:323
  86.9 12.2 %collective-permute-start.2 = (f32[4,256]{1,0:T(4,128)S(1)}, f32[4,256]{1,0:T(4,128)S(1)}, u32[]{:S(2)}, u32[]{:S(2)}) collective-permute-start(f32[4,256]{1,0:T(4,128)S(1)} %get-tuple-element.26), channel_id=1, source_target_pairs={{0,4},{4,8},{8,12},{12,16},{16,20},{20,24},{24,28},{28,32},{32,36}... | collective-permute-start | bytes 12296 | tf_op jit(solution)/shard_map/ppermute | solution.py:319
  90.5 8.7 %collective-permute-start.3 = (f32[4,256]{1,0:T(4,128)S(1)}, f32[4,256]{1,0:T(4,128)S(1)}, u32[]{:S(2)}, u32[]{:S(2)}) collective-permute-start(f32[4,256]{1,0:T(4,128)S(1)} %get-tuple-element.28), channel_id=1, source_target_pairs={{4,0},{8,4},{12,8},{16,12},{20,16},{24,20},{28,24},{32,28},{36,32}... | collective-permute-start | bytes 12296 | tf_op jit(solution)/shard_map/ppermute | solution.py:319
  99.2 1.7 %copy-start.4 = (f32[2,5,256,256]{3,2,1,0:T(8,128)S(1)}, f32[2,5,256,256]{3,2,1,0:T(8,128)}, u32[]{:S(2)}) copy-start(f32[2,5,256,256]{3,2,1,0:T(8,128)} %band_ref.5) | copy-start | bytes 7864324

commit v2 on v0

v2 whole, which is shorter than its diff:
```python
import functools

import jax
import jax.numpy as jnp
from jax import lax
from jax.experimental import pallas as pl
from jax.experimental.pallas import tpu as pltpu
from jax.sharding import Mesh, PartitionSpec as P

F32 = jnp.float32
I32 = jnp.int32
LANES = 128
CHUNK = 32
VMEM = pl.BlockSpec(memory_space=pltpu.VMEM)
SMEM = pl.BlockSpec(memory_space=pltpu.SMEM)
HBM = pl.BlockSpec(memory_space=pltpu.HBM)


def rows_iota(shape):
    return lax.broadcasted_iota(I32, shape, 0)


def lanes_iota(shape):
    return lax.broadcasted_iota(I32, shape, 1)


def columns_of(block_rows):
    n, width = block_rows.shape
    padded = jnp.concatenate([block_rows, jnp.zeros((LANES - n, width), F32)], axis=0)
    return jnp.transpose(padded)


def pick_lane(ref, start, lane):
    chunk = ref[start : start + CHUNK, :]
    return jnp.sum(jnp.where(lanes_iota(chunk.shape) == lane, chunk, 0.0), axis=1, keepdims=True)


def fold(chunk):
    total = chunk[0:8]
    for at in range(8, chunk.shape[0], 8):
        total = total + chunk[at : at + 8]
    return total


def put_lane(ref, start, lane, column):
    hit = lanes_iota((CHUNK, LANES)) == lane
    ref[start : start + CHUNK, :] += jnp.where(hit, column, 0.0)


def band_columns(band_ref, cols_scr, sums_scr, anchor, ready):
    blk_dev, spans, width, _ = band_ref.shape
    sums_scr[...] = jnp.zeros(sums_scr.shape, F32)

    def one(q, carry):
        ready(q)
        sums = [jnp.zeros((8, width), F32) for _ in range(spans)]
        for start in range(0, width, CHUNK):
            here = pick_lane(cols_scr, start, anchor + q)
            for k in range(spans):
                chunk = band_ref[q, k, start : start + CHUNK, :]
                if k == 0:
                    above = rows_iota(chunk.shape) + start < lanes_iota(chunk.shape)
                    chunk = jnp.where(above, chunk, 0.0)
                sums[k] = sums[k] + fold(chunk * here)
        for k in range(spans):
            sums_scr[pl.ds(anchor + q + k, 1), :] += jnp.sum(sums[k], axis=0, keepdims=True)
        return carry

    lax.fori_loop(0, blk_dev, one, 0)


def band_rows(band_ref, ext_scr, racc_scr, anchor):
    blk_dev, spans, width, _ = band_ref.shape

    def one(q, carry):
        biases = [ext_scr[pl.ds(anchor + q + k, 1), :] for k in range(spans)]
        for start in range(0, width, CHUNK):
            total = jnp.zeros((CHUNK, width), F32)
            for k in range(spans):
                chunk = band_ref[q, k, start : start + CHUNK, :]
                if k == 0:
                    upper = rows_iota(chunk.shape) + start <= lanes_iota(chunk.shape)
                    chunk = jnp.where(upper, chunk, 0.0)
                total = total + chunk * biases[k]
            put_lane(racc_scr, start, anchor + q, jnp.sum(total, axis=1, keepdims=True))
        return carry

    lax.fori_loop(0, blk_dev, one, 0)


def trans_columns(trans_ref, info_ref, cols_scr, emit, ready):
    tiles, width, _ = trans_ref.shape

    def one(t, carry):
        ready(t)
        total = jnp.zeros((8, width), F32)
        for start in range(0, width, CHUNK):
            here = pick_lane(cols_scr, start, info_ref[8 + t])
            total = total + fold(trans_ref[t, start : start + CHUNK, :] * here)
        emit(t, jnp.sum(total, axis=0, keepdims=True))
        return carry

    lax.fori_loop(0, tiles, one, 0)


def trans_rows(trans_ref, info_ref, bias_of, racc_scr):
    tiles, width, _ = trans_ref.shape

    def one(t, carry):
        near, far = bias_of(t)
        for start in range(0, width, CHUNK):
            chunk = trans_ref[t, start : start + CHUNK, :]
            total = chunk[:, :LANES] * near + chunk[:, LANES:] * far
            put_lane(racc_scr, start, info_ref[8 + t], jnp.sum(total, axis=1, keepdims=True))
        return carry

    lax.fori_loop(0, tiles, one, 0)


def add_sums(code_of, half_of, steps, blk_g):
    out = [[jnp.zeros((8, LANES), F32) for _ in range(2)] for _ in range(blk_g)]
    for step in steps:
        code = code_of(step)
        for h in range(2):
            piece = half_of(step, h)
            for c in range(blk_g):
                out[c][h] = out[c][h] + jnp.where(code == c + 1.0, piece, 0.0)
    sums = [[jnp.sum(half, axis=0, keepdims=True) for half in pair] for pair in out]
    return jnp.concatenate([jnp.concatenate(pair, axis=1) for pair in sums], axis=0)


def nothing(_):
    pass


def fill_send(bias, info_ref, band_ref, trans_ref, send_ref, part_ref, scratch, band_ready=nothing,
              trans_ready=nothing):
    cols_scr, sums_scr, flat_scr, spill_scr = scratch
    blk_g = bias.shape[0]
    blk_dev, spans = band_ref.shape[:2]
    slot = 2 * blk_g
    half = slot // 2
    reach = spans - 1
    chip, core = lax.axis_index("chip"), lax.axis_index("core")
    here = 2 * chip + core
    for h in range(2):
        flat_scr[pl.ds(h, blk_g, stride=2), :] = bias[:, LANES * h : LANES * h + LANES]
    cols_scr[...] = columns_of(bias)
    flat = flat_scr[...]
    for at in range(send_ref.shape[0] // slot):
        send_ref[slot * at : slot * at + slot, :] = jnp.where(at < chip, flat, 0.0)

    def emit(t, sums):
        base = slot * (info_ref[t] // 2)
        odd = info_ref[t] % 2
        code = jnp.where(info_ref[t] == here, 0, info_ref[16 + t] + 1).astype(F32)
        for h in range(2):
            send_ref[pl.ds(base + 2 * odd + h, 1), :] = sums[:, LANES * h : LANES * h + LANES]
        send_ref[pl.ds(base + 4 + odd, 1), :] = jnp.full((1, LANES), code, F32)

    trans_columns(trans_ref, info_ref, cols_scr, emit, trans_ready)
    anchor = lax.axis_index("rep") * blk_dev
    band_columns(band_ref, cols_scr, sums_scr, anchor, band_ready)
    part_ref[...] = sums_scr[0:blk_g, :]
    for h in range(2):
        part = sums_scr[blk_g : blk_g + reach, LANES * h : LANES * h + LANES]
        spill_scr[pl.ds(h, reach, stride=2), :] = part
    spill = spill_scr[...]
    mine = pl.multiple_of(slot * chip, slot)
    send_ref[pl.ds(mine, half), :] = flat[0:half]
    send_ref[pl.ds(mine + half, half), :] = spill

    @pl.when((core == 1) & (chip < lax.axis_size("chip") - 1))
    def _():
        send_ref[pl.ds(mine + slot + half, half), :] = spill


def first_kernel(masked_ref, cols_ref, rows_ref, count_ref, band_in, trans_in, own_ref, info_ref,
                 send_ref, part_ref, band_ref, trans_ref, sems, flat_scr, *scratch):
    blk_g = own_ref.shape[0]
    blk_dev, tiles = band_ref.shape[0], trans_ref.shape[0]

    def trans_copy(t):
        return pltpu.make_async_copy(trans_in.at[t], trans_ref.at[t], sems.at[t])

    def band_copy(q):
        return pltpu.make_async_copy(band_in.at[q], band_ref.at[q], sems.at[tiles + q])

    for t in range(tiles):
        trans_copy(t).start()
    for q in range(blk_dev):
        band_copy(q).start()
    here = 2 * lax.axis_index("chip") + lax.axis_index("core")
    for t in range(tiles):
        used = t < count_ref[0]
        target = cols_ref[t] // blk_g
        info_ref[t] = jnp.where(used, target, here)
        info_ref[8 + t] = jnp.where(used, rows_ref[t] - here * blk_g, LANES - 1)
        info_ref[16 + t] = cols_ref[t] - target * blk_g
    flat_scr[...] = 1.0 - masked_ref[...].astype(F32)
    own = jnp.concatenate([flat_scr[pl.ds(h, blk_g, stride=2), :] for h in range(2)], axis=1)
    own_ref[...] = own
    fill_send(own, info_ref, band_ref, trans_ref, send_ref, part_ref, scratch,
              lambda q: band_copy(q).wait(), lambda t: trans_copy(t).wait())


def spread(value, scr):
    scr[...] = value
    n = value.shape[0] // 2
    return jnp.concatenate([scr[pl.ds(h, n, stride=2), :] for h in range(2)], axis=1)


def fill_shares(share_ref, total):
    for s in range(share_ref.shape[0]):
        share_ref[s] = total


def meet_kernel(own_ref, part_ref, got_ref, mate_ref, info_ref, band_ref, trans_ref,
                share_ref, ext_scr, racc_scr, near_scr):
    blk_g, width = own_ref.shape
    blk_dev, spans = band_ref.shape[:2]
    reach = spans - 1
    slot = 2 * blk_g
    half = slot // 2
    chips = got_ref.shape[0] // slot
    chip, core = lax.axis_index("chip"), lax.axis_index("core")
    anchor = lax.axis_index("rep") * blk_dev
    first = core == 0
    at = pl.multiple_of(slot * jnp.minimum(chip + core, chips - 1), slot)
    ahead = jnp.where(chip + core < chips, mate_ref[pl.ds(at, half), :], 0.0)
    at = pl.multiple_of(slot * jnp.maximum(chip + core - 1, 0), slot)
    back = jnp.where(chip + core > 0, mate_ref[pl.ds(at + half, half), :], 0.0)
    ext_scr[0:blk_g, :] = own_ref[...]
    ext_scr[blk_g : blk_g + reach, :] = spread(ahead, near_scr)
    racc_scr[...] = jnp.zeros(racc_scr.shape, F32)
    band_rows(band_ref, ext_scr, racc_scr, anchor)

    def bias_of(t):
        source = info_ref[t]
        row = slot * (source // 2) + 2 * info_ref[16 + t]
        same = source % 2 == core
        return [
            jnp.where(same, got_ref[pl.ds(row + h, 1), :], mate_ref[pl.ds(row + h, 1), :])
            for h in range(2)
        ]

    trans_rows(trans_ref, info_ref, bias_of, racc_scr)

    def pick(ref, step, row):
        even, odd = row
        base = step * 8 * slot
        return jnp.where(
            first,
            ref[pl.ds(base + even, 8, stride=slot), :],
            ref[pl.ds(base + odd, 8, stride=slot), :],
        )

    steps = [(i, step) for i in range(2) for step in range(chips // 8)]
    refs = (got_ref, mate_ref)

    def code_of(which):
        i, step = which
        code = pick(refs[i], step, (4, 5))
        return jnp.where(rows_iota(code.shape) + 8 * step < chip, code, 0.0)

    sums = add_sums(code_of, lambda w, h: pick(refs[w[0]], w[1], (h, 2 + h)), steps, blk_g)
    total = part_ref[...] + jnp.transpose(racc_scr[...])[0:blk_g, :] + sums
    total = total + jnp.concatenate(
        [spread(back, near_scr), jnp.zeros((blk_g - reach, width), F32)], axis=0
    )
    fill_shares(share_ref, total)


def total_of(shares_ref):
    total = shares_ref[0]
    for s in range(1, shares_ref.shape[0]):
        total = total + shares_ref[s]
    return total


def second_kernel(shares_ref, own_ref, info_ref, band_ref, trans_ref, bias_ref, first_ref, send_ref,
                  part_ref, *scratch):
    kept = own_ref[...] > 0.0
    total = total_of(shares_ref)
    bias = jnp.where(kept, 1.0 / jnp.where(kept, total, 1.0), 0.0)
    bias_ref[...] = bias
    first_ref[...] = jnp.where(kept, total, 0.0)
    fill_send(bias, info_ref, band_ref, trans_ref, send_ref, part_ref, scratch)


def whole_sum(block):
    return jnp.sum(jnp.sum(block, axis=0, keepdims=True), axis=1, keepdims=True)


def stats_kernel(shares_ref, own_ref, bias_ref, first_ref, second_ref, stats_ref):
    total = total_of(shares_ref)
    second_ref[...] = total
    count = whole_sum(own_ref[...])
    sum_one = whole_sum(first_ref[...])
    scale = sum_one / jnp.maximum(count, 1.0)
    scale = jnp.where(scale == 0.0, 1.0, scale)
    sum_two = whole_sum((bias_ref[...] * scale) * (total * scale))
    lane = lanes_iota(stats_ref.shape)
    stats = jnp.where(lane == 0, sum_one, 0.0)
    stats = jnp.where(lane == 1, sum_two, stats)
    stats = jnp.where(lane == 2, scale, stats)
    stats_ref[...] = jnp.where(lane == 3, count, stats)


def final_kernel(stats_ref, own_ref, bias_ref, second_ref, weights_ref, coverage_ref):
    stats = stats_ref[...]
    lane = lanes_iota(stats.shape)

    def lane_of(at):
        return jnp.sum(jnp.where(lane == at, stats, 0.0), axis=1, keepdims=True)

    count = jnp.sum(lane_of(3), axis=0, keepdims=True)
    average_one = jnp.sum(lane_of(0), axis=0, keepdims=True) / count
    ratio = average_one / lane_of(2)
    average_two = jnp.sum(lane_of(1) * ratio * ratio, axis=0, keepdims=True) / count
    own = own_ref[...]
    blk_g = own.shape[0]
    kept = own > 0.0
    total = second_ref[...] * average_one
    coverage = (bias_ref[...] * average_one) * total
    weights = jnp.where(kept, average_two / jnp.where(kept, total, 1.0), 0.0)
    for h in range(2):
        part = slice(LANES * h, LANES * h + LANES)
        weights_ref[pl.ds(h, blk_g, stride=2), :] = weights[:, part]
        coverage_ref[pl.ds(h, blk_g, stride=2), :] = coverage[:, part]


def call(kernel, ins, outs, scratch=(), cost=None, limit=16):
    return pl.pallas_call(
        kernel,
        in_specs=list(ins),
        out_shape=[jax.ShapeDtypeStruct(s, d) for s, d, _ in outs],
        out_specs=[spec for _, _, spec in outs],
        scratch_shapes=list(scratch),
        compiler_params=pltpu.CompilerParams(vmem_limit_bytes=limit * 1024 * 1024),
        cost_estimate=cost and pl.CostEstimate(flops=cost, bytes_accessed=cost, transcendentals=0),
    )


def floats(*shape):
    return (shape, F32, VMEM)


def exchange(block, axis):
    return lax.all_to_all(block, axis, 0, 0, tiled=True)


def swap_cores(block):
    return lax.ppermute(block, "core", [(0, 1), (1, 0)])


def shards(band, trans, rows_at, cols_at, trans_count, masked):
    blk_dev, spans, width, _ = band.shape
    tiles = trans.shape[0]
    replicas = lax.axis_size("rep")
    chips = lax.axis_size("chip")
    blk_g = blk_dev * replicas
    own_like = floats(blk_g, width)
    send_like = floats(chips * 2 * blk_g, LANES)
    cols_scr = pltpu.VMEM((width, LANES), F32)
    wide_scr = pltpu.VMEM((16, width), F32)
    flat_scr = pltpu.VMEM((2 * blk_g, LANES), F32)
    half_scr = pltpu.VMEM((2 * spans - 2, LANES), F32)
    fill_scr = [cols_scr, wide_scr, flat_scr, half_scr]
    own, info, send, part = call(
        first_kernel,
        [VMEM, SMEM, SMEM, SMEM, HBM, HBM],
        [own_like, ((24,), I32, SMEM), send_like, own_like],
        [pltpu.VMEM(band.shape, F32), pltpu.VMEM(trans.shape, F32),
         pltpu.SemaphoreType.DMA((tiles + blk_dev,)), flat_scr] + fill_scr,
        limit=52,
    )(masked.reshape(2 * blk_g, LANES), cols_at, rows_at, trans_count, band, trans)
    bias = own
    for sweep in range(2):
        got = exchange(send, "chip")
        mate = swap_cores(got)
        (share,) = call(
            meet_kernel,
            [VMEM, VMEM, VMEM, VMEM, SMEM, VMEM, VMEM],
            [floats(replicas, blk_g, width)],
            [wide_scr, cols_scr, half_scr],
        )(bias, part, got, mate, info, band, trans)
        shares = exchange(share, "rep")
        if not sweep:
            bias, first, send, part = call(
                second_kernel,
                [VMEM, VMEM, SMEM, VMEM, VMEM],
                [own_like, own_like, send_like, own_like],
                fill_scr,
            )(shares, own, info, band, trans)
    second, stats = call(
        stats_kernel, [VMEM] * 4, [own_like, floats(2 * chips, LANES)]
    )(shares, own, bias, first)
    stats = exchange(stats, GENOME)
    weights, coverage = call(
        final_kernel, [VMEM] * 4, [floats(2 * blk_g, LANES)] * 2
    )(stats, own, bias, second)
    return (weights.reshape(-1), coverage.reshape(-1))


GENOME = ("chip", "core")


def solution(mesh):
    names = mesh.axis_names
    groups, replicas = (mesh.shape[name] for name in ("genome", "rep"))
    assert names == ("genome", "rep")
    devices = mesh.devices.reshape(groups // 2, 2, replicas)
    split = Mesh(devices, GENOME + ("rep",))
    every = P(GENOME + ("rep",))
    out_specs = (P(GENOME), P(GENOME))
    return jax.shard_map(
        shards, mesh=split, in_specs=(every,) * 5 + (P(GENOME),), out_specs=out_specs, check_vma=False
    )
```

time: 1120 us -> 117 us (0.10)
  waiting for transfers between devices: 487 us -> 3.03 us
  blocking collectives: 519 us -> 86.9 us
  matrix products: 30.8 us -> 0 us
  starting transfers between devices: 33.8 us -> 12.6 us
  local copies, waits for them, and re-layouts: 22.8 us -> 2.01 us
  between operations: 17.4 us -> 1.33 us
    psum x4 -> x0, blocking collectives: 519 us -> none  [the longest x2 493 us: shards(): lax.psum((jnp.sum(coverage * unmasked), jnp.sum(unmasked)), 'genome')]
    reduce_scatter x2 -> x0, waiting for transfers between devices: 336 us -> none  [shards(): lax.psum_scatter(spread, 'genome', scatter_dimension=0, tiled=True)]
    all_gather x2 -> x0, waiting for transfers between devices: 151 us -> none  [shards(): every_bias = lax.all_gather(weights, 'genome', axis=0, tiled=True)]
    all_to_all x0 -> x5, blocking collectives: none -> 86.9 us  [exchange(): return lax.all_to_all(block, axis, 0, 0, tiled=True)]
    dot_general x16 -> x0, matrix products: 30.8 us -> none  [the longest x2 8.22 us: shards(): jnp.einsum('qkij,qkj->qi', masked_tiles, column_bias, precision=HIGH)]
    ppermute x4 -> x2, starting transfers between devices: 33.5 us -> 12.6 us  [swap_cores(): return lax.ppermute(block, 'core', [(0, 1), (1, 0)])]
    unnamed x13 -> x10, local copies, waits for them, and re-layouts: 17.7 us -> 2.01 us
  transfers between devices with their start and end apart: 8 -> 2, of which waited for: 6 -> 2; matrix products, arithmetic and copies ran while one was open for 5% -> 0% of each run, Pallas kernels for 0% -> 0%
where the time goes in v2:
time: 117 us; the launch traced here: 116 us
  blocking collectives  86.9 us (74%)
  starting transfers between devices  12.6 us (11%)
  Pallas kernels  10.4 us (9%)
  waiting for transfers between devices  3.03 us (3%)
  local copies, waits for them, and re-layouts  2.01 us (2%)
  between operations  1.33 us (1%)
    all_to_all x5, blocking collectives, exchange(): return lax.all_to_all(block, axis, 0, 0, tiled=True)  86.9 us
    ppermute x2, starting transfers between devices, swap_cores(): return lax.ppermute(block, 'core', [(0, 1), (1, 0)])  12.6 us
    pallas_call x1, Pallas kernels, shards(): call(first_kernel, [VMEM, SMEM, SMEM, SMEM, HBM, HBM], [own_like, ((24,),...  4.01 us
    pallas_call x2, Pallas kernels, shards(): call(meet_kernel, [VMEM, VMEM, VMEM, VMEM, SMEM, VMEM, VMEM], [floats(rep...  3.68 us
    ppermute x2, waiting for transfers between devices, swap_cores(): return lax.ppermute(block, 'core', [(0, 1), (1, 0)])  3.03 us
  transfers between devices with their start and end apart: 2, of which 2 were waited for; matrix products, arithmetic and copies ran while one was open for 0% of the time, Pallas kernels for 0%

profile of v2, /device:TPU:1, one launch (start us, length us, event | category | flops | bytes accessed | tf_op | source)
XLA Modules:
  0.0 116.3 jit_solution(11953061979496154355)
XLA Ops:
  1.3 0.0 copy-start.2
  1.3 0.7 copy-done.2
  2.0 0.0 copy-start.3
  2.0 0.7 copy-done.3
  2.6 0.0 copy-start.4
  2.6 0.7 copy-done.4
  3.3 0.0 copy-start
  3.3 0.0 copy-start.1
  3.3 4.0 %shard_map.77 = (f32[8,256]{1,0:T(8,128)S(1)}, s32[24]{0:T(128)S(1)}, f32[1024,128]{1,0:T(8,128)S(1)}, f32[8,256]{1,0:T(8,128)S(1)}) custom-call(s32[16,128]{1,0:T(8,128)S(1)} %bitcast.19, s32[6]{0:T(128)S(1)} %copy-done.3, s32[6]{0:T(128)S(1)} %copy-done.4, s32[1]{0:T(128)S(6)} %copy.9.count_ref, f32[2,5,256,256]{3,2,1,0:T(8,128)} %band_ref.5, ...), custom_call_target="tpu_custom_call" | custom-call | tf_op jit(solution)/shard_map/pallas_call | solution.py:370
  7.3 33.3 %all_to_all.43 = f32[64,16,128]{2,1,0:T(8,128)S(1)} all-to-all(f32[64,16,128]{2,1,0:T(8,128)S(1)} %bitcast.15), channel_id=1, replica_groups=mesh['chip'=64,'core'=2,'rep'=4] {'chip'}, dimensions={0} | all-to-all | bytes 1048576 | tf_op jit(solution)/shard_map/all_to_all | solution.py:350
  40.6 5.8 %collective-permute-start = (f32[1024,128]{1,0:T(8,128)S(1)}, f32[1024,128]{1,0:T(8,128)S(1)}, u32[]{:S(2)}, u32[]{:S(2)}) collective-permute-start(f32[1024,128]{1,0:T(8,128)S(1)} %bitcast.11), channel_id=1, source_target_pairs={{0,4},{4,0},{1,5},{5,1},{2,6},{6,2},{3,7},{7,3},{8,12},{12,8},{9,1... | collective-permute-start | bytes 1572872 | tf_op jit(solution)/shard_map/ppermute | solution.py:354
  46.4 1.5 %collective-permute-done.mate_ref = f32[1024,128]{1,0:T(8,128)S(1)} collective-permute-done((f32[1024,128]{1,0:T(8,128)S(1)}, f32[1024,128]{1,0:T(8,128)S(1)}, u32[]{:S(2)}, u32[]{:S(2)}) %collective-permute-start) | collective-permute-done | bytes 524320 | tf_op jit(solution)/shard_map/ppermute | solution.py:354
  47.9 0.0 copy-done
  47.9 0.0 copy-done.1
  47.9 1.8 %shard_map.78 = f32[4,8,256]{2,1,0:T(8,128)S(1)} custom-call(f32[8,256]{1,0:T(8,128)S(1)} %get-tuple-element.14.own_ref, f32[8,256]{1,0:T(8,128)S(1)} %get-tuple-element.15.part_ref, f32[1024,128]{1,0:T(8,128)S(1)} %bitcast.12, f32[1024,128]{1,0:T(8,128)S(1)} %collective-permute-done.mate_ref, s32[24]{0:T(128)S(1)} %get-tuple-element.17.info_ref, ...), custom_call_target="tpu_custom_call" | custom-call | tf_op jit(solution)/shard_map/pallas_call | solution.py:382
  49.8 8.1 %all_to_all.44.shares_ref = f32[4,8,256]{2,1,0:T(8,128)S(1)} all-to-all(f32[4,8,256]{2,1,0:T(8,128)S(1)} %shard_map.78), channel_id=1, replica_groups=mesh['chip'=64,'core'=2,'rep'=4] {'rep'}, dimensions={0} | all-to-all | bytes 65536 | tf_op jit(solution)/shard_map/all_to_all | solution.py:350
  57.9 1.8 %shard_map.79 = (f32[8,256]{1,0:T(8,128)S(1)}, f32[8,256]{1,0:T(8,128)S(1)}, f32[1024,128]{1,0:T(8,128)S(1)}, f32[8,256]{1,0:T(8,128)S(1)}) custom-call(f32[4,8,256]{2,1,0:T(8,128)S(1)} %all_to_all.44.shares_ref, f32[8,256]{1,0:T(8,128)S(1)} %get-tuple-element.14.own_ref, s32[24]{0:T(128)S(1)} %get-tuple-element.17.info_ref, f32[2,5,256,256]{3,2,1,0:T(8,128)S(1)} %copy-done, ...), custom_call_target="tpu_custom_call" | custom-call | tf_op jit(solution)/shard_map/pallas_call | solution.py:390
  59.7 20.3 %all_to_all.45 = f32[64,16,128]{2,1,0:T(8,128)S(1)} all-to-all(f32[64,16,128]{2,1,0:T(8,128)S(1)} %bitcast.16), channel_id=1, replica_groups=mesh['chip'=64,'core'=2,'rep'=4] {'chip'}, dimensions={0} | all-to-all | bytes 1048576 | tf_op jit(solution)/shard_map/all_to_all | solution.py:350
  80.0 6.8 %collective-permute-start.1 = (f32[1024,128]{1,0:T(8,128)S(1)}, f32[1024,128]{1,0:T(8,128)S(1)}, u32[]{:S(2)}, u32[]{:S(2)}) collective-permute-start(f32[1024,128]{1,0:T(8,128)S(1)} %bitcast.13), channel_id=1, source_target_pairs={{0,4},{4,0},{1,5},{5,1},{2,6},{6,2},{3,7},{7,3},{8,12},{12,8},{9,1... | collective-permute-start | bytes 1572872 | tf_op jit(solution)/shard_map/ppermute | solution.py:354
  86.9 1.5 %collective-permute-done.1.mate_ref = f32[1024,128]{1,0:T(8,128)S(1)} collective-permute-done((f32[1024,128]{1,0:T(8,128)S(1)}, f32[1024,128]{1,0:T(8,128)S(1)}, u32[]{:S(2)}, u32[]{:S(2)}) %collective-permute-start.1) | collective-permute-done | bytes 524320 | tf_op jit(solution)/shard_map/ppermute | solution.py:354
  88.4 1.8 %shard_map.80 = f32[4,8,256]{2,1,0:T(8,128)S(1)} custom-call(f32[8,256]{1,0:T(8,128)S(1)} %get-tuple-element.18.own_ref.bias_ref, f32[8,256]{1,0:T(8,128)S(1)} %get-tuple-element.19.part_ref, f32[1024,128]{1,0:T(8,128)S(1)} %bitcast.14, f32[1024,128]{1,0:T(8,128)S(1)} %collective-permute-done.1.mate_ref, s32[24]{0:T(128)S(1)} %get-tuple-element.17.info_ref, ...), custom_call_target="tpu_custom_call" | custom-call | tf_op jit(solution)/shard_map/pallas_call | solution.py:382
  90.2 6.7 %all_to_all.46.shares_ref = f32[4,8,256]{2,1,0:T(8,128)S(1)} all-to-all(f32[4,8,256]{2,1,0:T(8,128)S(1)} %shard_map.80), channel_id=1, replica_groups=mesh['chip'=64,'core'=2,'rep'=4] {'rep'}, dimensions={0} | all-to-all | bytes 65536 | tf_op jit(solution)/shard_map/all_to_all | solution.py:350
  96.9 0.2 shard_map.81
  97.1 18.5 %all_to_all.47 = f32[128,1,128]{2,1,0:T(1,128)S(1)} all-to-all(f32[128,1,128]{2,1,0:T(1,128)S(1)} %bitcast.18), channel_id=1, replica_groups=mesh['chip'=64,'core'=2,'rep'=4] {'chip','core'}, dimensions={0} | all-to-all | bytes 131072 | tf_op jit(solution)/shard_map/all_to_all | solution.py:350
  115.6 0.8 shard_map.82
Async XLA Ops:
  1.3 0.7 copy-start.2
  2.0 0.7 copy-start.3
  2.6 0.7 copy-start.4
  3.3 44.6 %copy-start = (f32[2,5,256,256]{3,2,1,0:T(8,128)S(1)}, f32[2,5,256,256]{3,2,1,0:T(8,128)}, u32[]{:S(2)}) copy-start(f32[2,5,256,256]{3,2,1,0:T(8,128)} %band_ref.5) | copy-start | bytes 7864324
  3.3 44.6 %copy-start.1 = (f32[6,256,256]{2,1,0:T(8,128)S(1)}, f32[6,256,256]{2,1,0:T(8,128)}, u32[]{:S(2)}) copy-start(f32[6,256,256]{2,1,0:T(8,128)} %trans_ref.5) | copy-start | bytes 4718596
  40.6 7.3 %collective-permute-start = (f32[1024,128]{1,0:T(8,128)S(1)}, f32[1024,128]{1,0:T(8,128)S(1)}, u32[]{:S(2)}, u32[]{:S(2)}) collective-permute-start(f32[1024,128]{1,0:T(8,128)S(1)} %bitcast.11), channel_id=1, source_target_pairs={{0,4},{4,0},{1,5},{5,1},{2,6},{6,2},{3,7},{7,3},{8,12},{12,8},{9,1... | collective-permute-start | bytes 1572872 | tf_op jit(solution)/shard_map/ppermute | solution.py:354
  80.0 8.4 %collective-permute-start.1 = (f32[1024,128]{1,0:T(8,128)S(1)}, f32[1024,128]{1,0:T(8,128)S(1)}, u32[]{:S(2)}, u32[]{:S(2)}) collective-permute-start(f32[1024,128]{1,0:T(8,128)S(1)} %bitcast.13), channel_id=1, source_target_pairs={{0,4},{4,0},{1,5},{5,1},{2,6},{6,2},{3,7},{7,3},{8,12},{12,8},{9,1... | collective-permute-start | bytes 1572872 | tf_op jit(solution)/shard_map/ppermute | solution.py:354

commit v3 on v2

--- a/solution.py
+++ b/solution.py
@@ -210,13 +210,8 @@
     return jnp.concatenate([scr[pl.ds(h, n, stride=2), :] for h in range(2)], axis=1)
 
 
-def fill_shares(share_ref, total):
-    for s in range(share_ref.shape[0]):
-        share_ref[s] = total
-
-
 def meet_kernel(own_ref, part_ref, got_ref, mate_ref, info_ref, band_ref, trans_ref,
-                share_ref, ext_scr, racc_scr, near_scr):
+                share_ref, code_ref, ext_scr, racc_scr, near_scr):
     blk_g, width = own_ref.shape
     blk_dev, spans = band_ref.shape[:2]
     reach = spans - 1
@@ -264,42 +259,146 @@
         return jnp.where(rows_iota(code.shape) + 8 * step < chip, code, 0.0)
 
     sums = add_sums(code_of, lambda w, h: pick(refs[w[0]], w[1], (h, 2 + h)), steps, blk_g)
+    for i in range(2):
+        code = got_ref[pl.ds(4 + i, chips, stride=slot), :]
+        code_ref[i] = jnp.where(rows_iota(code.shape) < chip, code, 0.0)
     total = part_ref[...] + jnp.transpose(racc_scr[...])[0:blk_g, :] + sums
     total = total + jnp.concatenate(
         [spread(back, near_scr), jnp.zeros((blk_g - reach, width), F32)], axis=0
     )
-    fill_shares(share_ref, total)
-
-
-def total_of(shares_ref):
+    total = jnp.where(own_ref[...] > 0.0, total, jnp.inf)
+    for s in range(share_ref.shape[0]):
+        share_ref[s] = total
+
+
+def halves(block):
+    return [block[:, LANES * h : LANES * h + LANES] for h in range(2)]
+
+
+def second_kernel(shares_ref, code_ref, info_ref, band_ref, trans_ref, ext_ref, first_ref, send_ref,
+                  part_ref, cols_scr, sums_scr, spill_scr, ahead_scr):
+    blk_g = first_ref.shape[0]
+    blk_dev, spans = band_ref.shape[:2]
+    reach = spans - 1
+    replicas = shares_ref.shape[0] // 2
+    chips = send_ref.shape[0] // STEP
+    chip, core = lax.axis_index("chip"), lax.axis_index("core")
+    first = core == 0
+    totals, biases = [], []
+    for c in range(2):
+        total = shares_ref[c * replicas]
+        for s in range(1, replicas):
+            total = total + shares_ref[c * replicas + s]
+        kept = total != jnp.inf
+        totals.append(jnp.where(kept, total, 0.0))
+        biases.append(jnp.where(kept, 1.0 / jnp.where(kept, total, 1.0), 0.0))
+    first_ref[...] = jnp.where(first, totals[0], totals[1])
+    own = jnp.where(first, biases[0], biases[1])
+    ext_ref[0:blk_g, :] = own
+    ext_ref[blk_g : blk_g + reach, :] = biases[1][0:reach]
+    ext_ref[blk_g + reach :, :] = jnp.zeros((ext_ref.shape[0] - blk_g - reach, own.shape[1]), F32)
+    cols_scr[...] = columns_of(own)
+    for at in range(0, send_ref.shape[0], 8):
+        send_ref[at : at + 8, :] = jnp.zeros((8, LANES), F32)
+    for i in range(2):
+        pieces = halves(biases[i])
+        for at in range(0, chips, 8):
+            code = code_ref[i, at : at + 8, :]
+            for h in range(2):
+                piece = jnp.zeros((8, LANES), F32)
+                for c in range(blk_g):
+                    piece = jnp.where(code == c + 1.0, pieces[h][c : c + 1], piece)
+                send_ref[pl.ds(STEP * at + 2 - 2 * i + h, 8, stride=STEP), :] = piece
+
+    def emit(t, sums):
+        base = STEP * (info_ref[t] // 2) + 2 - 2 * (info_ref[t] % 2)
+        for h in range(2):
+            send_ref[pl.ds(base + h, 1), :] = halves(sums)[h]
+
+    trans_columns(trans_ref, info_ref, cols_scr, emit, nothing)
+    band_columns(band_ref, cols_scr, sums_scr, lax.axis_index("rep") * blk_dev, nothing)
+    spill = sums_scr[blk_g : blk_g + reach, :]
+    part_ref[0:blk_g, :] = sums_scr[0:blk_g, :]
+    mate = jnp.concatenate([spill, jnp.zeros((blk_g - reach, own.shape[1]), F32)], axis=0)
+    part_ref[blk_g : 2 * blk_g, :] = jnp.where(first, mate, 0.0)
+    for h in range(2):
+        spill_scr[pl.ds(h, reach, stride=2), :] = halves(spill)[h]
+        ahead_scr[pl.ds(h, reach, stride=2), :] = halves(biases[0])[h][0:reach]
+
+    @pl.when((core == 1) & (chip > 0))
+    def _():
+        for i in range(2 * reach):
+            send_ref[pl.ds(STEP * (chip - 1) + 2 + i, 1), :] = ahead_scr[i : i + 1, :]
+
+    @pl.when((core == 1) & (chip < chips - 1))
+    def _():
+        for i in range(2 * reach):
+            send_ref[pl.ds(STEP * (chip + 1) + 2 + i, 1), :] = spill_scr[i : i + 1, :]
+
+
+def third_kernel(code_ref, got_ref, ext_ref, part_ref, info_ref, band_ref, trans_ref, share_ref,
+                 ext_scr, racc_scr, near_scr):
+    blk_g = part_ref.shape[0] // 2
+    blk_dev, spans = band_ref.shape[:2]
+    reach = spans - 1
+    replicas = share_ref.shape[0] // 2
+    chips = got_ref.shape[0] // STEP
+    chip, core = lax.axis_index("chip"), lax.axis_index("core")
+    first = core == 0
+    ext_scr[...] = ext_ref[...]
+    racc_scr[...] = jnp.zeros(racc_scr.shape, F32)
+
+    def edge(at, valid):
+        at = jnp.clip(at, 0, chips - 1)
+        for i in range(2 * reach):
+            near_scr[i : i + 1, :] = got_ref[pl.ds(STEP * at + 2 + i, 1), :]
+        block = jnp.concatenate([near_scr[pl.ds(h, reach, stride=2), :] for h in range(2)], axis=1)
+        return jnp.where(valid, block, 0.0)
+
+    ahead = edge(chip + 1, chip + 1 < chips)
+    ext_scr[blk_g : blk_g + reach, :] = jnp.where(first, ext_ref[blk_g : blk_g + reach, :], ahead)
+    back = edge(chip - 1, (core == 1) & (chip > 0))
+    band_rows(band_ref, ext_scr, racc_scr, lax.axis_index("rep") * blk_dev)
+
+    def bias_of(t):
+        base = STEP * (info_ref[t] // 2) + 2 - 2 * (info_ref[t] % 2)
+        return [got_ref[pl.ds(base + h, 1), :] for h in range(2)]
+
+    trans_rows(trans_ref, info_ref, bias_of, racc_scr)
+    sums = [
+        add_sums(
+            lambda at: code_ref[i, at : at + 8, :],
+            lambda at, h: got_ref[pl.ds(STEP * at + 2 - 2 * i + h, 8, stride=STEP), :],
+            range(0, chips, 8),
+            blk_g,
+        )
+        for i in range(2)
+    ]
+    own = part_ref[0:blk_g, :] + jnp.transpose(racc_scr[...])[0:blk_g, :]
+    own = own + jnp.where(first, sums[0], sums[1])
+    mate = part_ref[blk_g : 2 * blk_g, :] + jnp.where(first, sums[1], sums[0])
+    mate = mate + jnp.concatenate([back, jnp.zeros((blk_g - reach, own.shape[1]), F32)], axis=0)
+    for c in range(2):
+        block = jnp.where(core == c, own, mate)
+        for s in range(replicas):
+            share_ref[c * replicas + s] = block
+
+
+def whole_sum(block):
+    return jnp.sum(jnp.sum(block, axis=0, keepdims=True), axis=1, keepdims=True)
+
+
+def stats_kernel(shares_ref, own_ref, ext_ref, first_ref, second_ref, stats_ref):
+    bias = ext_ref[0 : own_ref.shape[0], :]
     total = shares_ref[0]
     for s in range(1, shares_ref.shape[0]):
         total = total + shares_ref[s]
-    return total
-
-
-def second_kernel(shares_ref, own_ref, info_ref, band_ref, trans_ref, bias_ref, first_ref, send_ref,
-                  part_ref, *scratch):
-    kept = own_ref[...] > 0.0
-    total = total_of(shares_ref)
-    bias = jnp.where(kept, 1.0 / jnp.where(kept, total, 1.0), 0.0)
-    bias_ref[...] = bias
-    first_ref[...] = jnp.where(kept, total, 0.0)
-    fill_send(bias, info_ref, band_ref, trans_ref, send_ref, part_ref, scratch)
-
-
-def whole_sum(block):
-    return jnp.sum(jnp.sum(block, axis=0, keepdims=True), axis=1, keepdims=True)
-
-
-def stats_kernel(shares_ref, own_ref, bias_ref, first_ref, second_ref, stats_ref):
-    total = total_of(shares_ref)
     second_ref[...] = total
     count = whole_sum(own_ref[...])
     sum_one = whole_sum(first_ref[...])
     scale = sum_one / jnp.maximum(count, 1.0)
     scale = jnp.where(scale == 0.0, 1.0, scale)
-    sum_two = whole_sum((bias_ref[...] * scale) * (total * scale))
+    sum_two = whole_sum((bias * scale) * (total * scale))
     lane = lanes_iota(stats_ref.shape)
     stats = jnp.where(lane == 0, sum_one, 0.0)
     stats = jnp.where(lane == 1, sum_two, stats)
@@ -307,7 +406,7 @@
     stats_ref[...] = jnp.where(lane == 3, count, stats)
 
 
-def final_kernel(stats_ref, own_ref, bias_ref, second_ref, weights_ref, coverage_ref):
+def final_kernel(stats_ref, own_ref, ext_ref, second_ref, weights_ref, coverage_ref):
     stats = stats_ref[...]
     lane = lanes_iota(stats.shape)
 
@@ -322,7 +421,7 @@
     blk_g = own.shape[0]
     kept = own > 0.0
     total = second_ref[...] * average_one
-    coverage = (bias_ref[...] * average_one) * total
+    coverage = (ext_ref[0:blk_g, :] * average_one) * total
     weights = jnp.where(kept, average_two / jnp.where(kept, total, 1.0), 0.0)
     for h in range(2):
         part = slice(LANES * h, LANES * h + LANES)
@@ -362,6 +461,7 @@
     blk_g = blk_dev * replicas
     own_like = floats(blk_g, width)
     send_like = floats(chips * 2 * blk_g, LANES)
+    share_like = floats(2 * replicas, blk_g, width)
     cols_scr = pltpu.VMEM((width, LANES), F32)
     wide_scr = pltpu.VMEM((16, width), F32)
     flat_scr = pltpu.VMEM((2 * blk_g, LANES), F32)
@@ -375,35 +475,42 @@
          pltpu.SemaphoreType.DMA((tiles + blk_dev,)), flat_scr] + fill_scr,
         limit=52,
     )(masked.reshape(2 * blk_g, LANES), cols_at, rows_at, trans_count, band, trans)
-    bias = own
-    for sweep in range(2):
-        got = exchange(send, "chip")
-        mate = swap_cores(got)
-        (share,) = call(
-            meet_kernel,
-            [VMEM, VMEM, VMEM, VMEM, SMEM, VMEM, VMEM],
-            [floats(replicas, blk_g, width)],
-            [wide_scr, cols_scr, half_scr],
-        )(bias, part, got, mate, info, band, trans)
-        shares = exchange(share, "rep")
-        if not sweep:
-            bias, first, send, part = call(
-                second_kernel,
-                [VMEM, VMEM, SMEM, VMEM, VMEM],
-                [own_like, own_like, send_like, own_like],
-                fill_scr,
-            )(shares, own, info, band, trans)
+    got = exchange(send, "chip")
+    mate = swap_cores(got)
+    share, code = call(
+        meet_kernel,
+        [VMEM, VMEM, VMEM, VMEM, SMEM, VMEM, VMEM],
+        [share_like, floats(2, chips, LANES)],
+        [wide_scr, cols_scr, half_scr],
+    )(own, part, got, mate, info, band, trans)
+    shares = exchange(share, LOCAL)
+    ext, first, send, part = call(
+        second_kernel,
+        [VMEM, VMEM, SMEM, VMEM, VMEM],
+        [floats(16, width), own_like, floats(STEP * chips, LANES), floats(2 * blk_g, width)],
+        [cols_scr, wide_scr, half_scr, half_scr],
+    )(shares, code, info, band, trans)
+    got = exchange(send.reshape(STEP * chips // 2, 2, LANES), "chip").reshape(send.shape)
+    (share,) = call(
+        third_kernel,
+        [VMEM, VMEM, VMEM, VMEM, SMEM, VMEM, VMEM],
+        [share_like],
+        [wide_scr, cols_scr, half_scr],
+    )(code, got, ext, part, info, band, trans)
+    shares = exchange(share, LOCAL)
     second, stats = call(
         stats_kernel, [VMEM] * 4, [own_like, floats(2 * chips, LANES)]
-    )(shares, own, bias, first)
+    )(shares, own, ext, first)
     stats = exchange(stats, GENOME)
     weights, coverage = call(
         final_kernel, [VMEM] * 4, [floats(2 * blk_g, LANES)] * 2
-    )(stats, own, bias, second)
+    )(stats, own, ext, second)
     return (weights.reshape(-1), coverage.reshape(-1))
 
 
 GENOME = ("chip", "core")
+LOCAL = ("core", "rep")
+STEP = 10
 
 
 def solution(mesh):

time: 117 us -> 110 us (0.940)
  starting transfers between devices: 12.6 us -> 5.78 us
  waiting for transfers between devices: 3.03 us -> 1.51 us
  blocking collectives: 86.9 us -> 88.2 us
    ppermute x2 -> x1, starting transfers between devices: 12.6 us -> 5.78 us  [swap_cores(): return lax.ppermute(block, 'core', [(0, 1), (1, 0)])]
    ppermute x2 -> x1, waiting for transfers between devices: 3.03 us -> 1.51 us  [swap_cores(): return lax.ppermute(block, 'core', [(0, 1), (1, 0)])]
    all_to_all x5, blocking collectives: 86.9 us -> 88.2 us  [exchange(): return lax.all_to_all(block, axis, 0, 0, tiled=True)]
  transfers between devices with their start and end apart: 2 -> 1, of which waited for: 2 -> 1; matrix products, arithmetic and copies ran while one was open for 0% -> 0% of each run, Pallas kernels for 0% -> 0%
where the time goes in v3:
time: 110 us; the launch traced here: 109 us
  blocking collectives  88.2 us (80%)
  Pallas kernels  10.4 us (9%)
  starting transfers between devices  5.78 us (5%)
  local copies, waits for them, and re-layouts  2.01 us (2%)
  waiting for transfers between devices  1.51 us (1%)
  between operations  1.33 us (1%)
    all_to_all x5, blocking collectives, exchange(): return lax.all_to_all(block, axis, 0, 0, tiled=True)  88.2 us
    ppermute x1, starting transfers between devices, swap_cores(): return lax.ppermute(block, 'core', [(0, 1), (1, 0)])  5.78 us
    pallas_call x1, Pallas kernels, shards(): call(first_kernel, [VMEM, SMEM, SMEM, SMEM, HBM, HBM], [own_like, ((24,),...  4.01 us
  transfers between devices with their start and end apart: 1, of which 1 were waited for; matrix products, arithmetic and copies ran while one was open for 0% of the time, Pallas kernels for 0%

profile of v3, /device:TPU:1, one launch (start us, length us, event | category | flops | bytes accessed | tf_op | source)
XLA Modules:
  0.0 109.3 jit_solution(4616516712572622245)
XLA Ops:
  1.3 0.0 copy-start.2
  1.3 0.7 copy-done.2
  2.0 0.0 copy-start.3
  2.0 0.7 copy-done.3
  2.6 0.0 copy-start.4
  2.6 0.7 copy-done.4
  3.3 0.0 copy-start
  3.3 0.0 copy-start.1
  3.3 4.0 %shard_map.77 = (f32[8,256]{1,0:T(8,128)S(1)}, s32[24]{0:T(128)S(1)}, f32[1024,128]{1,0:T(8,128)S(1)}, f32[8,256]{1,0:T(8,128)S(1)}) custom-call(s32[16,128]{1,0:T(8,128)S(1)} %bitcast.18, s32[6]{0:T(128)S(1)} %copy-done.3, s32[6]{0:T(128)S(1)} %copy-done.4, s32[1]{0:T(128)S(6)} %copy.9.count_ref, f32[2,5,256,256]{3,2,1,0:T(8,128)} %band_ref.5, ...), custom_call_target="tpu_custom_call" | custom-call | tf_op jit(solution)/shard_map/pallas_call | solution.py:470
  7.3 33.3 %all_to_all.37 = f32[64,16,128]{2,1,0:T(8,128)S(1)} all-to-all(f32[64,16,128]{2,1,0:T(8,128)S(1)} %bitcast.14), channel_id=1, replica_groups=mesh['chip'=64,'core'=2,'rep'=4] {'chip'}, dimensions={0} | all-to-all | bytes 1048576 | tf_op jit(solution)/shard_map/all_to_all | solution.py:449
  40.6 5.8 %collective-permute-start = (f32[1024,128]{1,0:T(8,128)S(1)}, f32[1024,128]{1,0:T(8,128)S(1)}, u32[]{:S(2)}, u32[]{:S(2)}) collective-permute-start(f32[1024,128]{1,0:T(8,128)S(1)} %bitcast.11), channel_id=1, source_target_pairs={{0,4},{4,0},{1,5},{5,1},{2,6},{6,2},{3,7},{7,3},{8,12},{12,8},{9,1... | collective-permute-start | bytes 1572872 | tf_op jit(solution)/shard_map/ppermute | solution.py:453
  46.4 1.5 %collective-permute-done.mate_ref = f32[1024,128]{1,0:T(8,128)S(1)} collective-permute-done((f32[1024,128]{1,0:T(8,128)S(1)}, f32[1024,128]{1,0:T(8,128)S(1)}, u32[]{:S(2)}, u32[]{:S(2)}) %collective-permute-start) | collective-permute-done | bytes 524320 | tf_op jit(solution)/shard_map/ppermute | solution.py:453
  47.9 0.0 copy-done
  47.9 0.0 copy-done.1
  47.9 1.9 %shard_map.78 = (f32[8,8,256]{2,1,0:T(8,128)S(1)}, f32[2,64,128]{2,1,0:T(8,128)S(1)}) custom-call(f32[8,256]{1,0:T(8,128)S(1)} %get-tuple-element.16.own_ref, f32[8,256]{1,0:T(8,128)S(1)} %get-tuple-element.17.part_ref, f32[1024,128]{1,0:T(8,128)S(1)} %bitcast.12, f32[1024,128]{1,0:T(8,128)S(1)} %collective-permute-done.mate_ref, ...), custom_call_target="tpu_custom_call" | custom-call | tf_op jit(solution)/shard_map/pallas_call | solution.py:480
  49.8 9.4 %all_to_all.38.shares_ref = f32[8,8,256]{2,1,0:T(8,128)S(1)} all-to-all(f32[8,8,256]{2,1,0:T(8,128)S(1)} %get-tuple-element.21), channel_id=1, replica_groups=mesh['chip'=64,'core'=2,'rep'=4] {'core','rep'}, dimensions={0} | all-to-all | bytes 131072 | tf_op jit(solution)/shard_map/all_to_all | solution.py:449
  59.2 1.8 %shard_map.79 = (f32[16,256]{1,0:T(8,128)S(1)}, f32[8,256]{1,0:T(8,128)S(1)}, f32[640,128]{1,0:T(8,128)S(1)}, f32[16,256]{1,0:T(8,128)S(1)}) custom-call(f32[8,8,256]{2,1,0:T(8,128)S(1)} %all_to_all.38.shares_ref, f32[2,64,128]{2,1,0:T(8,128)S(1)} %get-tuple-element.20.code_ref, s32[24]{0:T(128)S(1)} %get-tuple-element.19.info_ref, ...), custom_call_target="tpu_custom_call" | custom-call | tf_op jit(solution)/shard_map/pallas_call | solution.py:487
  61.0 19.0 %all_to_all.39 = f32[320,2,128]{2,1,0:T(2,128)S(1)} all-to-all(f32[320,2,128]{2,1,0:T(2,128)S(1)} %bitcast.15), channel_id=1, replica_groups=mesh['chip'=64,'core'=2,'rep'=4] {'chip'}, dimensions={0} | all-to-all | bytes 655360 | tf_op jit(solution)/shard_map/all_to_all | solution.py:449
  80.0 1.8 %shard_map.80 = f32[8,8,256]{2,1,0:T(8,128)S(1)} custom-call(f32[2,64,128]{2,1,0:T(8,128)S(1)} %get-tuple-element.20.code_ref, f32[640,128]{1,0:T(8,128)S(1)} %bitcast.13, f32[16,256]{1,0:T(8,128)S(1)} %get-tuple-element.23.ext_ref, f32[16,256]{1,0:T(8,128)S(1)} %get-tuple-element.24.part_ref, s32[24]{0:T(128)S(1)} %get-tuple-element.19.info_ref, ...), custom_call_target="tpu_custom_call" | custom-call | tf_op jit(solution)/shard_map/pallas_call | solution.py:494
  81.8 10.0 %all_to_all.40.shares_ref = f32[8,8,256]{2,1,0:T(8,128)S(1)} all-to-all(f32[8,8,256]{2,1,0:T(8,128)S(1)} %shard_map.80), channel_id=1, replica_groups=mesh['chip'=64,'core'=2,'rep'=4] {'core','rep'}, dimensions={0} | all-to-all | bytes 131072 | tf_op jit(solution)/shard_map/all_to_all | solution.py:449
  91.7 0.2 shard_map.81
  91.9 16.6 %all_to_all.41 = f32[128,1,128]{2,1,0:T(1,128)S(1)} all-to-all(f32[128,1,128]{2,1,0:T(1,128)S(1)} %bitcast.17), channel_id=1, replica_groups=mesh['chip'=64,'core'=2,'rep'=4] {'chip','core'}, dimensions={0} | all-to-all | bytes 131072 | tf_op jit(solution)/shard_map/all_to_all | solution.py:449
  108.5 0.8 shard_map.82
Async XLA Ops:
  1.3 0.7 copy-start.2
  2.0 0.7 copy-start.3
  2.6 0.7 copy-start.4
  3.3 44.6 %copy-start = (f32[2,5,256,256]{3,2,1,0:T(8,128)S(1)}, f32[2,5,256,256]{3,2,1,0:T(8,128)}, u32[]{:S(2)}) copy-start(f32[2,5,256,256]{3,2,1,0:T(8,128)} %band_ref.5) | copy-start | bytes 7864324
  3.3 44.6 %copy-start.1 = (f32[6,256,256]{2,1,0:T(8,128)S(1)}, f32[6,256,256]{2,1,0:T(8,128)}, u32[]{:S(2)}) copy-start(f32[6,256,256]{2,1,0:T(8,128)} %trans_ref.5) | copy-start | bytes 4718596
  40.6 7.3 %collective-permute-start = (f32[1024,128]{1,0:T(8,128)S(1)}, f32[1024,128]{1,0:T(8,128)S(1)}, u32[]{:S(2)}, u32[]{:S(2)}) collective-permute-start(f32[1024,128]{1,0:T(8,128)S(1)} %bitcast.11), channel_id=1, source_target_pairs={{0,4},{4,0},{1,5},{5,1},{2,6},{6,2},{3,7},{7,3},{8,12},{12,8},{9,1... | collective-permute-start | bytes 1572872 | tf_op jit(solution)/shard_map/ppermute | solution.py:453

commit v4 on v3

--- a/solution.py
+++ b/solution.py
@@ -14,6 +14,7 @@
 VMEM = pl.BlockSpec(memory_space=pltpu.VMEM)
 SMEM = pl.BlockSpec(memory_space=pltpu.SMEM)
 HBM = pl.BlockSpec(memory_space=pltpu.HBM)
+ANY = pl.BlockSpec(memory_space=pl.ANY)
 
 
 def rows_iota(shape):
@@ -66,7 +67,7 @@
             sums_scr[pl.ds(anchor + q + k, 1), :] += jnp.sum(sums[k], axis=0, keepdims=True)
         return carry
 
-    lax.fori_loop(0, blk_dev, one, 0)
+    lax.fori_loop(0, blk_dev, one, 0, unroll=True)
 
 
 def band_rows(band_ref, ext_scr, racc_scr, anchor):
@@ -85,7 +86,7 @@
             put_lane(racc_scr, start, anchor + q, jnp.sum(total, axis=1, keepdims=True))
         return carry
 
-    lax.fori_loop(0, blk_dev, one, 0)
+    lax.fori_loop(0, blk_dev, one, 0, unroll=True)
 
 
 def trans_columns(trans_ref, info_ref, cols_scr, emit, ready):
@@ -100,7 +101,7 @@
         emit(t, jnp.sum(total, axis=0, keepdims=True))
         return carry
 
-    lax.fori_loop(0, tiles, one, 0)
+    lax.fori_loop(0, tiles, one, 0, unroll=True)
 
 
 def trans_rows(trans_ref, info_ref, bias_of, racc_scr):
@@ -114,7 +115,7 @@
             put_lane(racc_scr, start, info_ref[8 + t], jnp.sum(total, axis=1, keepdims=True))
         return carry
 
-    lax.fori_loop(0, tiles, one, 0)
+    lax.fori_loop(0, tiles, one, 0, unroll=True)
 
 
 def add_sums(code_of, half_of, steps, blk_g):
@@ -133,8 +134,14 @@
     pass
 
 
-def fill_send(bias, info_ref, band_ref, trans_ref, send_ref, part_ref, scratch, band_ready=nothing,
-              trans_ready=nothing):
+def quotient(value, size):
+    if size & (size - 1):
+        return lax.div(value, size)
+    return lax.shift_right_logical(value, size.bit_length() - 1)
+
+
+def fill_send(bias, info_ref, band_ref, trans_ref, send_ref, part_ref, scratch, band_ready,
+              trans_ready):
     cols_scr, sums_scr, flat_scr, spill_scr = scratch
     blk_g = bias.shape[0]
     blk_dev, spans = band_ref.shape[:2]
@@ -151,8 +158,8 @@
         send_ref[slot * at : slot * at + slot, :] = jnp.where(at < chip, flat, 0.0)
 
     def emit(t, sums):
-        base = slot * (info_ref[t] // 2)
-        odd = info_ref[t] % 2
+        base = slot * quotient(info_ref[t], 2)
+        odd = info_ref[t] & 1
         code = jnp.where(info_ref[t] == here, 0, info_ref[16 + t] + 1).astype(F32)
         for h in range(2):
             send_ref[pl.ds(base + 2 * odd + h, 1), :] = sums[:, LANES * h : LANES * h + LANES]
@@ -175,33 +182,53 @@
         send_ref[pl.ds(mine + slot + half, half), :] = spill
 
 
-def first_kernel(masked_ref, cols_ref, rows_ref, count_ref, band_in, trans_in, own_ref, info_ref,
-                 send_ref, part_ref, band_ref, trans_ref, sems, flat_scr, *scratch):
+def first_kernel(count_ref, masked_in, cols_in, rows_in, band_in, trans_in, own_ref, info_ref, send_ref,
+                 part_ref, band_ref, trans_ref, masked_ref, cols_ref, rows_ref, sems, tile_sems,
+                 flat_scr, *scratch):
     blk_g = own_ref.shape[0]
     blk_dev, tiles = band_ref.shape[0], trans_ref.shape[0]
-
-    def trans_copy(t):
-        return pltpu.make_async_copy(trans_in.at[t], trans_ref.at[t], sems.at[t])
+    small = [
+        pltpu.make_async_copy(src, dst, sems.at[i])
+        for i, (src, dst) in enumerate(
+            ((cols_in, cols_ref), (rows_in, rows_ref), (masked_in, masked_ref))
+        )
+    ]
+
+    some = tiles // 2 if tiles % 2 == 0 else tiles
+
+    def trans_copy(i):
+        part = pl.ds(some * i, some)
+        return pltpu.make_async_copy(trans_in.at[part], trans_ref.at[part], tile_sems.at[i])
 
     def band_copy(q):
-        return pltpu.make_async_copy(band_in.at[q], band_ref.at[q], sems.at[tiles + q])
-
-    for t in range(tiles):
-        trans_copy(t).start()
+        return pltpu.make_async_copy(band_in.at[q], band_ref.at[q], tile_sems.at[tiles + q])
+
+    for copy in small:
+        copy.start()
+    for i in range(tiles // some):
+        trans_copy(i).start(priority=i % 2)
     for q in range(blk_dev):
-        band_copy(q).start()
+        band_copy(q).start(priority=q % 2)
+    for copy in small:
+        copy.wait()
     here = 2 * lax.axis_index("chip") + lax.axis_index("core")
     for t in range(tiles):
         used = t < count_ref[0]
-        target = cols_ref[t] // blk_g
+        target = quotient(cols_ref[t], blk_g)
         info_ref[t] = jnp.where(used, target, here)
         info_ref[8 + t] = jnp.where(used, rows_ref[t] - here * blk_g, LANES - 1)
         info_ref[16 + t] = cols_ref[t] - target * blk_g
     flat_scr[...] = 1.0 - masked_ref[...].astype(F32)
     own = jnp.concatenate([flat_scr[pl.ds(h, blk_g, stride=2), :] for h in range(2)], axis=1)
     own_ref[...] = own
+
+    def trans_ready(t):
+        @pl.when(t % some == 0)
+        def _():
+            trans_copy(t // some).wait()
+
     fill_send(own, info_ref, band_ref, trans_ref, send_ref, part_ref, scratch,
-              lambda q: band_copy(q).wait(), lambda t: trans_copy(t).wait())
+              lambda q: band_copy(q).wait(), trans_ready)
 
 
 def spread(value, scr):
@@ -210,8 +237,10 @@
     return jnp.concatenate([scr[pl.ds(h, n, stride=2), :] for h in range(2)], axis=1)
 
 
-def meet_kernel(own_ref, part_ref, got_ref, mate_ref, info_ref, band_ref, trans_ref,
-                share_ref, code_ref, ext_scr, racc_scr, near_scr):
+def meet_kernel(own_ref, part_ref, got_ref, mate_ref, info_in, band_ref, trans_ref,
+                share_ref, code_ref, info_ref, info_sem, ext_scr, racc_scr, near_scr):
+    table = pltpu.make_async_copy(info_in, info_ref, info_sem)
+    table.start()
     blk_g, width = own_ref.shape
     blk_dev, spans = band_ref.shape[:2]
     reach = spans - 1
@@ -229,11 +258,12 @@
     ext_scr[blk_g : blk_g + reach, :] = spread(ahead, near_scr)
     racc_scr[...] = jnp.zeros(racc_scr.shape, F32)
     band_rows(band_ref, ext_scr, racc_scr, anchor)
+    table.wait()
 
     def bias_of(t):
         source = info_ref[t]
-        row = slot * (source // 2) + 2 * info_ref[16 + t]
-        same = source % 2 == core
+        row = slot * quotient(source, 2) + 2 * info_ref[16 + t]
+        same = (source & 1) == core
         return [
             jnp.where(same, got_ref[pl.ds(row + h, 1), :], mate_ref[pl.ds(row + h, 1), :])
             for h in range(2)
@@ -275,8 +305,10 @@
     return [block[:, LANES * h : LANES * h + LANES] for h in range(2)]
 
 
-def second_kernel(shares_ref, code_ref, info_ref, band_ref, trans_ref, ext_ref, first_ref, send_ref,
-                  part_ref, cols_scr, sums_scr, spill_scr, ahead_scr):
+def second_kernel(shares_ref, code_ref, info_in, band_ref, trans_ref, ext_ref, first_ref, send_ref,
+                  part_ref, info_ref, info_sem, cols_scr, sums_scr, spill_scr, ahead_scr):
+    table = pltpu.make_async_copy(info_in, info_ref, info_sem)
+    table.start()
     blk_g = first_ref.shape[0]
     blk_dev, spans = band_ref.shape[:2]
     reach = spans - 1
@@ -298,8 +330,6 @@
     ext_ref[blk_g : blk_g + reach, :] = biases[1][0:reach]
     ext_ref[blk_g + reach :, :] = jnp.zeros((ext_ref.shape[0] - blk_g - reach, own.shape[1]), F32)
     cols_scr[...] = columns_of(own)
-    for at in range(0, send_ref.shape[0], 8):
-        send_ref[at : at + 8, :] = jnp.zeros((8, LANES), F32)
     for i in range(2):
         pieces = halves(biases[i])
         for at in range(0, chips, 8):
@@ -311,12 +341,13 @@
                 send_ref[pl.ds(STEP * at + 2 - 2 * i + h, 8, stride=STEP), :] = piece
 
     def emit(t, sums):
-        base = STEP * (info_ref[t] // 2) + 2 - 2 * (info_ref[t] % 2)
+        base = STEP * quotient(info_ref[t], 2) + 2 - 2 * (info_ref[t] & 1)
         for h in range(2):
             send_ref[pl.ds(base + h, 1), :] = halves(sums)[h]
 
+    band_columns(band_ref, cols_scr, sums_scr, lax.axis_index("rep") * blk_dev, nothing)
+    table.wait()
     trans_columns(trans_ref, info_ref, cols_scr, emit, nothing)
-    band_columns(band_ref, cols_scr, sums_scr, lax.axis_index("rep") * blk_dev, nothing)
     spill = sums_scr[blk_g : blk_g + reach, :]
     part_ref[0:blk_g, :] = sums_scr[0:blk_g, :]
     mate = jnp.concatenate([spill, jnp.zeros((blk_g - reach, own.shape[1]), F32)], axis=0)
@@ -336,8 +367,10 @@
             send_ref[pl.ds(STEP * (chip + 1) + 2 + i, 1), :] = spill_scr[i : i + 1, :]
 
 
-def third_kernel(code_ref, got_ref, ext_ref, part_ref, info_ref, band_ref, trans_ref, share_ref,
-                 ext_scr, racc_scr, near_scr):
+def third_kernel(code_ref, got_ref, ext_ref, part_ref, info_in, band_ref, trans_ref, share_ref,
+                 info_ref, info_sem, ext_scr, racc_scr, near_scr):
+    table = pltpu.make_async_copy(info_in, info_ref, info_sem)
+    table.start()
     blk_g = part_ref.shape[0] // 2
     blk_dev, spans = band_ref.shape[:2]
     reach = spans - 1
@@ -359,9 +392,10 @@
     ext_scr[blk_g : blk_g + reach, :] = jnp.where(first, ext_ref[blk_g : blk_g + reach, :], ahead)
     back = edge(chip - 1, (core == 1) & (chip > 0))
     band_rows(band_ref, ext_scr, racc_scr, lax.axis_index("rep") * blk_dev)
+    table.wait()
 
     def bias_of(t):
-        base = STEP * (info_ref[t] // 2) + 2 - 2 * (info_ref[t] % 2)
+        base = STEP * quotient(info_ref[t], 2) + 2 - 2 * (info_ref[t] & 1)
         return [got_ref[pl.ds(base + h, 1), :] for h in range(2)]
 
     trans_rows(trans_ref, info_ref, bias_of, racc_scr)
@@ -466,36 +500,55 @@
     wide_scr = pltpu.VMEM((16, width), F32)
     flat_scr = pltpu.VMEM((2 * blk_g, LANES), F32)
     half_scr = pltpu.VMEM((2 * spans - 2, LANES), F32)
+    info_scr = [pltpu.SMEM((24,), I32), pltpu.SemaphoreType.DMA(())]
     fill_scr = [cols_scr, wide_scr, flat_scr, half_scr]
-    own, info, send, part = call(
+    masked, cols_at, rows_at, band, trans = (
+        pltpu.with_memory_space_constraint(x, pltpu.HBM)
+        for x in (masked.reshape(2 * blk_g, LANES), cols_at, rows_at, band, trans)
+    )
+    own, info, send, part, band, trans = pl.pallas_call(
         first_kernel,
-        [VMEM, SMEM, SMEM, SMEM, HBM, HBM],
-        [own_like, ((24,), I32, SMEM), send_like, own_like],
-        [pltpu.VMEM(band.shape, F32), pltpu.VMEM(trans.shape, F32),
-         pltpu.SemaphoreType.DMA((tiles + blk_dev,)), flat_scr] + fill_scr,
-        limit=52,
-    )(masked.reshape(2 * blk_g, LANES), cols_at, rows_at, trans_count, band, trans)
+        in_specs=[SMEM] + [HBM] * 5,
+        out_shape=[
+            jax.ShapeDtypeStruct((blk_g, width), F32),
+            jax.ShapeDtypeStruct((24,), I32),
+            jax.ShapeDtypeStruct((chips * 2 * blk_g, LANES), F32),
+            jax.ShapeDtypeStruct((blk_g, width), F32),
+            pltpu.VMEM(band.shape, F32),
+            pltpu.VMEM(trans.shape, F32),
+        ],
+        out_specs=[VMEM, SMEM, VMEM, VMEM, VMEM, VMEM],
+        scratch_shapes=[
+            pltpu.VMEM((2 * blk_g, LANES), I32),
+            pltpu.SMEM((tiles,), I32),
+            pltpu.SMEM((tiles,), I32),
+            pltpu.SemaphoreType.DMA((3,)),
+            pltpu.SemaphoreType.DMA((tiles + blk_dev,)),
+            flat_scr,
+        ] + fill_scr,
+        compiler_params=pltpu.CompilerParams(vmem_limit_bytes=16 * 1024 * 1024),
+    )(trans_count, masked, cols_at, rows_at, band, trans)
     got = exchange(send, "chip")
     mate = swap_cores(got)
     share, code = call(
         meet_kernel,
-        [VMEM, VMEM, VMEM, VMEM, SMEM, VMEM, VMEM],
+        [VMEM, VMEM, VMEM, VMEM, ANY, VMEM, VMEM],
         [share_like, floats(2, chips, LANES)],
-        [wide_scr, cols_scr, half_scr],
+        info_scr + [wide_scr, cols_scr, half_scr],
     )(own, part, got, mate, info, band, trans)
     shares = exchange(share, LOCAL)
     ext, first, send, part = call(
         second_kernel,
-        [VMEM, VMEM, SMEM, VMEM, VMEM],
+        [VMEM, VMEM, ANY, VMEM, VMEM],
         [floats(16, width), own_like, floats(STEP * chips, LANES), floats(2 * blk_g, width)],
-        [cols_scr, wide_scr, half_scr, half_scr],
+        info_scr + [cols_scr, wide_scr, half_scr, half_scr],
     )(shares, code, info, band, trans)
     got = exchange(send.reshape(STEP * chips // 2, 2, LANES), "chip").reshape(send.shape)
     (share,) = call(
         third_kernel,
-        [VMEM, VMEM, VMEM, VMEM, SMEM, VMEM, VMEM],
+        [VMEM, VMEM, VMEM, VMEM, ANY, VMEM, VMEM],
         [share_like],
-        [wide_scr, cols_scr, half_scr],
+        info_scr + [wide_scr, cols_scr, half_scr],
     )(code, got, ext, part, info, band, trans)
     shares = exchange(share, LOCAL)
     second, stats = call(

time: 110 us -> 104 us (0.945)
  Pallas kernels: 10.4 us -> 7.08 us
  local copies, waits for them, and re-layouts: 2.01 us -> 0 us
    pallas_call x4, Pallas kernels: 9.48 us -> 6.14 us  [the longest x1 3.1 us: shards(): pl.pallas_call(first_kernel, in_specs=[SMEM] + [HBM] * 5, out_shape=[jax....]
    unnamed x10 -> x0, local copies, waits for them, and re-layouts: 2.01 us -> none
where the time goes in v4:
time: 104 us
  blocking collectives  88.2 us (85%)
  Pallas kernels  7.08 us (7%)
  starting transfers between devices  5.78 us (6%)
  waiting for transfers between devices  1.51 us (1%)
  between operations  1.32 us (1%)
    all_to_all x5, blocking collectives, exchange(): return lax.all_to_all(block, axis, 0, 0, tiled=True)  88.2 us
    ppermute x1, starting transfers between devices, swap_cores(): return lax.ppermute(block, 'core', [(0, 1), (1, 0)])  5.78 us
    pallas_call x1, Pallas kernels, shards(): pl.pallas_call(first_kernel, in_specs=[SMEM] + [HBM] * 5, out_shape=[jax....  3.1 us
  transfers between devices with their start and end apart: 1, of which 1 were waited for; matrix products, arithmetic and copies ran while one was open for 0% of the time, Pallas kernels for 0%

profile of v4, /device:TPU:1, one launch (start us, length us, event | category | flops | bytes accessed | tf_op | source)
XLA Modules:
  0.0 103.9 jit_solution(16820259083043256098)
XLA Ops:
  1.3 3.1 %shard_map.77 = (f32[8,256]{1,0:T(8,128)S(1)}, s32[24]{0:T(128)S(1)}, f32[1024,128]{1,0:T(8,128)S(1)}, f32[8,256]{1,0:T(8,128)S(1)}, f32[2,5,256,256]{3,2,1,0:T(8,128)S(1)}, /*index=5*/f32[6,256,256]{2,1,0:T(8,128)S(1)}) custom-call(s32[1]{0:T(128)S(6)} %copy.9.count_ref, s32[16,128]{1,0:T(8,128)} %bitcast.18, s32[6]{0:T(128)} %cols_in.1, s32[6]{0:T(128)} %rows_in.1, ...), custom_call_target="tpu_custom_call" | custom-call | tf_op jit(solution)/shard_map/pallas_call | solution.py:509
  4.4 33.3 %all_to_all.37 = f32[64,16,128]{2,1,0:T(8,128)S(1)} all-to-all(f32[64,16,128]{2,1,0:T(8,128)S(1)} %bitcast.14), channel_id=1, replica_groups=mesh['chip'=64,'core'=2,'rep'=4] {'chip'}, dimensions={0} | all-to-all | bytes 1048576 | tf_op jit(solution)/shard_map/all_to_all | solution.py:483
  37.7 5.8 %collective-permute-start = (f32[1024,128]{1,0:T(8,128)S(1)}, f32[1024,128]{1,0:T(8,128)S(1)}, u32[]{:S(2)}, u32[]{:S(2)}) collective-permute-start(f32[1024,128]{1,0:T(8,128)S(1)} %bitcast.11), channel_id=1, source_target_pairs={{0,4},{4,0},{1,5},{5,1},{2,6},{6,2},{3,7},{7,3},{8,12},{12,8},{9,1... | collective-permute-start | bytes 1572872 | tf_op jit(solution)/shard_map/ppermute | solution.py:487
  43.5 1.5 %collective-permute-done.mate_ref = f32[1024,128]{1,0:T(8,128)S(1)} collective-permute-done((f32[1024,128]{1,0:T(8,128)S(1)}, f32[1024,128]{1,0:T(8,128)S(1)}, u32[]{:S(2)}, u32[]{:S(2)}) %collective-permute-start) | collective-permute-done | bytes 524320 | tf_op jit(solution)/shard_map/ppermute | solution.py:487
  45.0 1.2 %shard_map.78 = (f32[8,8,256]{2,1,0:T(8,128)S(1)}, f32[2,64,128]{2,1,0:T(8,128)S(1)}) custom-call(f32[8,256]{1,0:T(8,128)S(1)} %get-tuple-element.18.own_ref, f32[8,256]{1,0:T(8,128)S(1)} %get-tuple-element.19.part_ref, f32[1024,128]{1,0:T(8,128)S(1)} %bitcast.12, f32[1024,128]{1,0:T(8,128)S(1)} %collective-permute-done.mate_ref, ...), custom_call_target="tpu_custom_call" | custom-call | tf_op jit(solution)/shard_map/pallas_call | solution.py:533
  46.2 9.4 %all_to_all.38.shares_ref = f32[8,8,256]{2,1,0:T(8,128)S(1)} all-to-all(f32[8,8,256]{2,1,0:T(8,128)S(1)} %get-tuple-element.25), channel_id=1, replica_groups=mesh['chip'=64,'core'=2,'rep'=4] {'core','rep'}, dimensions={0} | all-to-all | bytes 131072 | tf_op jit(solution)/shard_map/all_to_all | solution.py:483
  55.6 0.9 shard_map.79
  56.5 19.0 %all_to_all.39 = f32[320,2,128]{2,1,0:T(2,128)S(1)} all-to-all(f32[320,2,128]{2,1,0:T(2,128)S(1)} %bitcast.15), channel_id=1, replica_groups=mesh['chip'=64,'core'=2,'rep'=4] {'chip'}, dimensions={0} | all-to-all | bytes 655360 | tf_op jit(solution)/shard_map/all_to_all | solution.py:483
  75.5 1.0 shard_map.80
  76.4 10.0 %all_to_all.40.shares_ref = f32[8,8,256]{2,1,0:T(8,128)S(1)} all-to-all(f32[8,8,256]{2,1,0:T(8,128)S(1)} %shard_map.80), channel_id=1, replica_groups=mesh['chip'=64,'core'=2,'rep'=4] {'core','rep'}, dimensions={0} | all-to-all | bytes 131072 | tf_op jit(solution)/shard_map/all_to_all | solution.py:483
  86.4 0.2 shard_map.81
  86.6 16.6 %all_to_all.41 = f32[128,1,128]{2,1,0:T(1,128)S(1)} all-to-all(f32[128,1,128]{2,1,0:T(1,128)S(1)} %bitcast.17), channel_id=1, replica_groups=mesh['chip'=64,'core'=2,'rep'=4] {'chip','core'}, dimensions={0} | all-to-all | bytes 131072 | tf_op jit(solution)/shard_map/all_to_all | solution.py:483
  103.2 0.8 shard_map.82
Async XLA Ops:
  37.7 7.3 %collective-permute-start = (f32[1024,128]{1,0:T(8,128)S(1)}, f32[1024,128]{1,0:T(8,128)S(1)}, u32[]{:S(2)}, u32[]{:S(2)}) collective-permute-start(f32[1024,128]{1,0:T(8,128)S(1)} %bitcast.11), channel_id=1, source_target_pairs={{0,4},{4,0},{1,5},{5,1},{2,6},{6,2},{3,7},{7,3},{8,12},{12,8},{9,1... | collective-permute-start | bytes 1572872 | tf_op jit(solution)/shard_map/ppermute | solution.py:487

commit v5 on v4

--- a/solution.py
+++ b/solution.py
@@ -305,30 +305,49 @@
     return [block[:, LANES * h : LANES * h + LANES] for h in range(2)]
 
 
+def whole_sum(block):
+    return jnp.sum(jnp.sum(block, axis=0, keepdims=True), axis=1, keepdims=True)
+
+
+def in_lanes(shape, *values):
+    lane = lanes_iota(shape)
+    out = jnp.zeros(shape, F32)
+    for i, value in enumerate(values):
+        out = jnp.where(lane == i, value, out)
+    return out
+
+
+def lane_of(block, at):
+    return jnp.sum(jnp.where(lanes_iota(block.shape) == at, block, 0.0), axis=1, keepdims=True)
+
+
 def second_kernel(shares_ref, code_ref, info_in, band_ref, trans_ref, ext_ref, first_ref, send_ref,
                   part_ref, info_ref, info_sem, cols_scr, sums_scr, spill_scr, ahead_scr):
     table = pltpu.make_async_copy(info_in, info_ref, info_sem)
     table.start()
-    blk_g = first_ref.shape[0]
+    blk_g = shares_ref.shape[1]
     blk_dev, spans = band_ref.shape[:2]
     reach = spans - 1
     replicas = shares_ref.shape[0] // 2
     chips = send_ref.shape[0] // STEP
     chip, core = lax.axis_index("chip"), lax.axis_index("core")
     first = core == 0
-    totals, biases = [], []
+    biases, sums, counts = [], [], []
     for c in range(2):
         total = shares_ref[c * replicas]
         for s in range(1, replicas):
             total = total + shares_ref[c * replicas + s]
         kept = total != jnp.inf
-        totals.append(jnp.where(kept, total, 0.0))
+        sums.append(jnp.where(kept, total, 0.0))
+        counts.append(jnp.where(kept, 1.0, 0.0))
         biases.append(jnp.where(kept, 1.0 / jnp.where(kept, total, 1.0), 0.0))
-    first_ref[...] = jnp.where(first, totals[0], totals[1])
+    sum_one, count = whole_sum(sums[0] + sums[1]), whole_sum(counts[0] + counts[1])
+    scale = sum_one / jnp.maximum(count, 1.0)
+    scale = jnp.where(scale == 0.0, 1.0, scale)
+    first_ref[...] = in_lanes(first_ref.shape, sum_one, 0.0, scale, count)
     own = jnp.where(first, biases[0], biases[1])
     ext_ref[0:blk_g, :] = own
-    ext_ref[blk_g : blk_g + reach, :] = biases[1][0:reach]
-    ext_ref[blk_g + reach :, :] = jnp.zeros((ext_ref.shape[0] - blk_g - reach, own.shape[1]), F32)
+    ext_ref[blk_g:, :] = jnp.where(first, biases[1], biases[0])
     cols_scr[...] = columns_of(own)
     for i in range(2):
         pieces = halves(biases[i])
@@ -367,14 +386,14 @@
             send_ref[pl.ds(STEP * (chip + 1) + 2 + i, 1), :] = spill_scr[i : i + 1, :]
 
 
-def third_kernel(code_ref, got_ref, ext_ref, part_ref, info_in, band_ref, trans_ref, share_ref,
+def third_kernel(code_ref, got_ref, ext_ref, part_ref, first_ref, info_in, band_ref, trans_ref, share_ref,
                  info_ref, info_sem, ext_scr, racc_scr, near_scr):
     table = pltpu.make_async_copy(info_in, info_ref, info_sem)
     table.start()
     blk_g = part_ref.shape[0] // 2
     blk_dev, spans = band_ref.shape[:2]
     reach = spans - 1
-    replicas = share_ref.shape[0] // 2
+    replicas = share_ref.shape[0] // (2 * SHARE)
     chips = got_ref.shape[0] // STEP
     chip, core = lax.axis_index("chip"), lax.axis_index("core")
     first = core == 0
@@ -412,55 +431,43 @@
     own = own + jnp.where(first, sums[0], sums[1])
     mate = part_ref[blk_g : 2 * blk_g, :] + jnp.where(first, sums[1], sums[0])
     mate = mate + jnp.concatenate([back, jnp.zeros((blk_g - reach, own.shape[1]), F32)], axis=0)
+    scale = lane_of(first_ref[0:1, :], 2)
+    weighed = (ext_ref[0:blk_g, :] * scale) * (own * scale)
+    sum_two = whole_sum(weighed + (ext_ref[blk_g:, :] * scale) * (mate * scale))
     for c in range(2):
-        block = jnp.where(core == c, own, mate)
+        pieces = halves(jnp.where(core == c, own, mate))
         for s in range(replicas):
-            share_ref[c * replicas + s] = block
-
-
-def whole_sum(block):
-    return jnp.sum(jnp.sum(block, axis=0, keepdims=True), axis=1, keepdims=True)
-
-
-def stats_kernel(shares_ref, own_ref, ext_ref, first_ref, second_ref, stats_ref):
-    bias = ext_ref[0 : own_ref.shape[0], :]
-    total = shares_ref[0]
-    for s in range(1, shares_ref.shape[0]):
-        total = total + shares_ref[s]
-    second_ref[...] = total
-    count = whole_sum(own_ref[...])
-    sum_one = whole_sum(first_ref[...])
-    scale = sum_one / jnp.maximum(count, 1.0)
-    scale = jnp.where(scale == 0.0, 1.0, scale)
-    sum_two = whole_sum((bias * scale) * (total * scale))
-    lane = lanes_iota(stats_ref.shape)
-    stats = jnp.where(lane == 0, sum_one, 0.0)
-    stats = jnp.where(lane == 1, sum_two, stats)
-    stats = jnp.where(lane == 2, scale, stats)
-    stats_ref[...] = jnp.where(lane == 3, count, stats)
+            at = SHARE * (c * replicas + s)
+            for h in range(2):
+                share_ref[pl.ds(at + h, blk_g, stride=2), :] = pieces[h]
+            share_ref[at + 2 * blk_g : at + SHARE, :] = jnp.broadcast_to(sum_two, (2, LANES))
+
+
+def stats_kernel(shares_ref, first_ref, second_ref, stats_ref):
+    size = SHARE - 2
+    shares = [shares_ref[at : at + SHARE, :] for at in range(0, shares_ref.shape[0], SHARE)]
+    total = shares[0]
+    for share in shares[1:]:
+        total = total + share
+    second_ref[...] = total[0:size]
+    stats = jnp.where(lanes_iota((1, LANES)) == 1, total[size : size + 1], first_ref[0:1, :])
+    stats_ref[...] = jnp.broadcast_to(stats, stats_ref.shape)
 
 
 def final_kernel(stats_ref, own_ref, ext_ref, second_ref, weights_ref, coverage_ref):
     stats = stats_ref[...]
-    lane = lanes_iota(stats.shape)
-
-    def lane_of(at):
-        return jnp.sum(jnp.where(lane == at, stats, 0.0), axis=1, keepdims=True)
-
-    count = jnp.sum(lane_of(3), axis=0, keepdims=True)
-    average_one = jnp.sum(lane_of(0), axis=0, keepdims=True) / count
-    ratio = average_one / lane_of(2)
-    average_two = jnp.sum(lane_of(1) * ratio * ratio, axis=0, keepdims=True) / count
-    own = own_ref[...]
-    blk_g = own.shape[0]
-    kept = own > 0.0
-    total = second_ref[...] * average_one
-    coverage = (ext_ref[0:blk_g, :] * average_one) * total
-    weights = jnp.where(kept, average_two / jnp.where(kept, total, 1.0), 0.0)
+    count = jnp.sum(lane_of(stats, 3), axis=0, keepdims=True)
+    average_one = jnp.sum(lane_of(stats, 0), axis=0, keepdims=True) / count
+    ratio = average_one / lane_of(stats, 2)
+    average_two = jnp.sum(lane_of(stats, 1) * ratio * ratio, axis=0, keepdims=True) / count
+    blk_g = own_ref.shape[0]
+    owns, biases = halves(own_ref[...]), halves(ext_ref[0:blk_g, :])
     for h in range(2):
-        part = slice(LANES * h, LANES * h + LANES)
-        weights_ref[pl.ds(h, blk_g, stride=2), :] = weights[:, part]
-        coverage_ref[pl.ds(h, blk_g, stride=2), :] = coverage[:, part]
+        rows = pl.ds(h, blk_g, stride=2)
+        kept = owns[h] > 0.0
+        total = second_ref[rows, :] * average_one
+        coverage_ref[rows, :] = (biases[h] * average_one) * total
+        weights_ref[rows, :] = jnp.where(kept, average_two / jnp.where(kept, total, 1.0), 0.0)
 
 
 def call(kernel, ins, outs, scratch=(), cost=None, limit=16):
@@ -540,21 +547,22 @@
     ext, first, send, part = call(
         second_kernel,
         [VMEM, VMEM, ANY, VMEM, VMEM],
-        [floats(16, width), own_like, floats(STEP * chips, LANES), floats(2 * blk_g, width)],
+        [floats(2 * blk_g, width), floats(8, LANES), floats(STEP * chips, LANES),
+         floats(2 * blk_g, width)],
         info_scr + [cols_scr, wide_scr, half_scr, half_scr],
     )(shares, code, info, band, trans)
     got = exchange(send.reshape(STEP * chips // 2, 2, LANES), "chip").reshape(send.shape)
     (share,) = call(
         third_kernel,
-        [VMEM, VMEM, VMEM, VMEM, ANY, VMEM, VMEM],
-        [share_like],
+        [VMEM, VMEM, VMEM, VMEM, VMEM, ANY, VMEM, VMEM],
+        [floats(2 * replicas * SHARE, LANES)],
         info_scr + [wide_scr, cols_scr, half_scr],
-    )(code, got, ext, part, info, band, trans)
-    shares = exchange(share, LOCAL)
+    )(code, got, ext, part, first, info, band, trans)
+    shares = exchange(share.reshape(replicas * SHARE, 2, LANES), LOCAL).reshape(share.shape)
     second, stats = call(
-        stats_kernel, [VMEM] * 4, [own_like, floats(2 * chips, LANES)]
-    )(shares, own, ext, first)
-    stats = exchange(stats, GENOME)
+        stats_kernel, [VMEM, VMEM], [floats(2 * blk_g, LANES), floats(chips, LANES)]
+    )(shares, first)
+    stats = exchange(stats, "chip")
     weights, coverage = call(
         final_kernel, [VMEM] * 4, [floats(2 * blk_g, LANES)] * 2
     )(stats, own, ext, second)
@@ -564,6 +572,7 @@
 GENOME = ("chip", "core")
 LOCAL = ("core", "rep")
 STEP = 10
+SHARE = 18
 
 
 def solution(mesh):

time: 104 us -> 102 us (0.981)
  blocking collectives: 88.2 us -> 86.6 us
    all_to_all x5, blocking collectives: 88.2 us -> 86.6 us  [exchange(): return lax.all_to_all(block, axis, 0, 0, tiled=True)]
where the time goes in v5:
time: 102 us
  blocking collectives  86.6 us (85%)
  Pallas kernels  6.95 us (7%)
  starting transfers between devices  5.78 us (6%)
  waiting for transfers between devices  1.51 us (1%)
  between operations  1.32 us (1%)
    all_to_all x5, blocking collectives, exchange(): return lax.all_to_all(block, axis, 0, 0, tiled=True)  86.6 us
    ppermute x1, starting transfers between devices, swap_cores(): return lax.ppermute(block, 'core', [(0, 1), (1, 0)])  5.78 us
    pallas_call x1, Pallas kernels, shards(): pl.pallas_call(first_kernel, in_specs=[SMEM] + [HBM] * 5, out_shape=[jax....  3.1 us
  transfers between devices with their start and end apart: 1, of which 1 were waited for; matrix products, arithmetic and copies ran while one was open for 0% of the time, Pallas kernels for 0%

profile of v5, /device:TPU:1, one launch (start us, length us, event | category | flops | bytes accessed | tf_op | source)
XLA Modules:
  0.0 102.1 jit_solution(4612550774408450254)
XLA Ops:
  1.3 3.1 %shard_map.77 = (f32[8,256]{1,0:T(8,128)S(1)}, s32[24]{0:T(128)S(1)}, f32[1024,128]{1,0:T(8,128)S(1)}, f32[8,256]{1,0:T(8,128)S(1)}, f32[2,5,256,256]{3,2,1,0:T(8,128)S(1)}, /*index=5*/f32[6,256,256]{2,1,0:T(8,128)S(1)}) custom-call(s32[1]{0:T(128)S(6)} %copy.9.count_ref, s32[16,128]{1,0:T(8,128)} %bitcast.22, s32[6]{0:T(128)} %cols_in.1, s32[6]{0:T(128)} %rows_in.1, ...), custom_call_target="tpu_custom_call" | custom-call | tf_op jit(solution)/shard_map/pallas_call | solution.py:516
  4.4 33.3 %all_to_all.37 = f32[64,16,128]{2,1,0:T(8,128)S(1)} all-to-all(f32[64,16,128]{2,1,0:T(8,128)S(1)} %bitcast.16), channel_id=1, replica_groups=mesh['chip'=64,'core'=2,'rep'=4] {'chip'}, dimensions={0} | all-to-all | bytes 1048576 | tf_op jit(solution)/shard_map/all_to_all | solution.py:490
  37.7 5.8 %collective-permute-start = (f32[1024,128]{1,0:T(8,128)S(1)}, f32[1024,128]{1,0:T(8,128)S(1)}, u32[]{:S(2)}, u32[]{:S(2)}) collective-permute-start(f32[1024,128]{1,0:T(8,128)S(1)} %bitcast.13), channel_id=1, source_target_pairs={{0,4},{4,0},{1,5},{5,1},{2,6},{6,2},{3,7},{7,3},{8,12},{12,8},{9,1... | collective-permute-start | bytes 1572872 | tf_op jit(solution)/shard_map/ppermute | solution.py:494
  43.5 1.5 %collective-permute-done.mate_ref = f32[1024,128]{1,0:T(8,128)S(1)} collective-permute-done((f32[1024,128]{1,0:T(8,128)S(1)}, f32[1024,128]{1,0:T(8,128)S(1)}, u32[]{:S(2)}, u32[]{:S(2)}) %collective-permute-start) | collective-permute-done | bytes 524320 | tf_op jit(solution)/shard_map/ppermute | solution.py:494
  45.0 1.2 %shard_map.78 = (f32[8,8,256]{2,1,0:T(8,128)S(1)}, f32[2,64,128]{2,1,0:T(8,128)S(1)}) custom-call(f32[8,256]{1,0:T(8,128)S(1)} %get-tuple-element.18.own_ref, f32[8,256]{1,0:T(8,128)S(1)} %get-tuple-element.19.part_ref, f32[1024,128]{1,0:T(8,128)S(1)} %bitcast.14, f32[1024,128]{1,0:T(8,128)S(1)} %collective-permute-done.mate_ref, ...), custom_call_target="tpu_custom_call" | custom-call | tf_op jit(solution)/shard_map/pallas_call | solution.py:540
  46.2 9.4 %all_to_all.38.shares_ref = f32[8,8,256]{2,1,0:T(8,128)S(1)} all-to-all(f32[8,8,256]{2,1,0:T(8,128)S(1)} %get-tuple-element.25), channel_id=1, replica_groups=mesh['chip'=64,'core'=2,'rep'=4] {'core','rep'}, dimensions={0} | all-to-all | bytes 131072 | tf_op jit(solution)/shard_map/all_to_all | solution.py:490
  55.6 0.9 shard_map.79
  56.5 19.0 %all_to_all.39 = f32[320,2,128]{2,1,0:T(2,128)S(1)} all-to-all(f32[320,2,128]{2,1,0:T(2,128)S(1)} %bitcast.17), channel_id=1, replica_groups=mesh['chip'=64,'core'=2,'rep'=4] {'chip'}, dimensions={0} | all-to-all | bytes 655360 | tf_op jit(solution)/shard_map/all_to_all | solution.py:490
  75.5 1.0 shard_map.80
  76.5 10.0 %all_to_all.40 = f32[72,2,128]{2,1,0:T(2,128)S(1)} all-to-all(f32[72,2,128]{2,1,0:T(2,128)S(1)} %bitcast.19), channel_id=1, replica_groups=mesh['chip'=64,'core'=2,'rep'=4] {'core','rep'}, dimensions={0} | all-to-all | bytes 147456 | tf_op jit(solution)/shard_map/all_to_all | solution.py:490
  86.5 14.9 %all_to_all.41 = f32[64,1,128]{2,1,0:T(1,128)S(1)} all-to-all(f32[64,1,128]{2,1,0:T(1,128)S(1)} %bitcast.21), channel_id=1, replica_groups=mesh['chip'=64,'core'=2,'rep'=4] {'chip'}, dimensions={0} | all-to-all | bytes 65536 | tf_op jit(solution)/shard_map/all_to_all | solution.py:490
  101.4 0.7 shard_map.82
  (1 shorter events, 0.0 us)
Async XLA Ops:
  37.7 7.3 %collective-permute-start = (f32[1024,128]{1,0:T(8,128)S(1)}, f32[1024,128]{1,0:T(8,128)S(1)}, u32[]{:S(2)}, u32[]{:S(2)}) collective-permute-start(f32[1024,128]{1,0:T(8,128)S(1)} %bitcast.13), channel_id=1, source_target_pairs={{0,4},{4,0},{1,5},{5,1},{2,6},{6,2},{3,7},{7,3},{8,12},{12,8},{9,1... | collective-permute-start | bytes 1572872 | tf_op jit(solution)/shard_map/ppermute | solution.py:494

commit v6 on v5

--- a/solution.py
+++ b/solution.py
@@ -535,7 +535,7 @@
         ] + fill_scr,
         compiler_params=pltpu.CompilerParams(vmem_limit_bytes=16 * 1024 * 1024),
     )(trans_count, masked, cols_at, rows_at, band, trans)
-    got = exchange(send, "chip")
+    got = exchange(send.reshape(chips, 1, 2 * blk_g * LANES), "chip").reshape(send.shape)
     mate = swap_cores(got)
     share, code = call(
         meet_kernel,

time: 102 us -> 102 us (level)
  no operation moved by 1% of the time
where the time goes in v6:
time: 102 us
  blocking collectives  86.6 us (85%)
  Pallas kernels  6.95 us (7%)
  starting transfers between devices  5.78 us (6%)
  waiting for transfers between devices  1.51 us (1%)
  between operations  1.32 us (1%)
    all_to_all x5, blocking collectives, exchange(): return lax.all_to_all(block, axis, 0, 0, tiled=True)  86.6 us
    ppermute x1, starting transfers between devices, swap_cores(): return lax.ppermute(block, 'core', [(0, 1), (1, 0)])  5.78 us
    pallas_call x1, Pallas kernels, shards(): pl.pallas_call(first_kernel, in_specs=[SMEM] + [HBM] * 5, out_shape=[jax....  3.1 us
  transfers between devices with their start and end apart: 1, of which 1 were waited for; matrix products, arithmetic and copies ran while one was open for 0% of the time, Pallas kernels for 0%

profile of v6, /device:TPU:1, one launch (start us, length us, event | category | flops | bytes accessed | tf_op | source)
XLA Modules:
  0.0 102.1 jit_solution(4612550774408450254)
XLA Ops:
  1.3 3.1 %shard_map.77 = (f32[8,256]{1,0:T(8,128)S(1)}, s32[24]{0:T(128)S(1)}, f32[1024,128]{1,0:T(8,128)S(1)}, f32[8,256]{1,0:T(8,128)S(1)}, f32[2,5,256,256]{3,2,1,0:T(8,128)S(1)}, /*index=5*/f32[6,256,256]{2,1,0:T(8,128)S(1)}) custom-call(s32[1]{0:T(128)S(6)} %copy.10.count_ref, s32[16,128]{1,0:T(8,128)} %bitcast.22, s32[6]{0:T(128)} %cols_in.1, s32[6]{0:T(128)} %rows_in.1, ...), custom_call_target="tpu_custom_call" | custom-call | tf_op jit(solution)/shard_map/pallas_call | solution.py:516
  4.4 33.3 %all_to_all.31 = f32[64,1,2048]{2,1,0:T(1,128)S(1)} all-to-all(f32[64,1,2048]{2,1,0:T(1,128)S(1)} %bitcast.16), channel_id=1, replica_groups=mesh['chip'=64,'core'=2,'rep'=4] {'chip'}, dimensions={0} | all-to-all | bytes 1048576 | tf_op jit(solution)/shard_map/all_to_all | solution.py:490
  37.7 5.8 %collective-permute-start = (f32[1024,128]{1,0:T(8,128)S(1)}, f32[1024,128]{1,0:T(8,128)S(1)}, u32[]{:S(2)}, u32[]{:S(2)}) collective-permute-start(f32[1024,128]{1,0:T(8,128)S(1)} %bitcast.13), channel_id=1, source_target_pairs={{0,4},{4,0},{1,5},{5,1},{2,6},{6,2},{3,7},{7,3},{8,12},{12,8},{9,1... | collective-permute-start | bytes 1572872 | tf_op jit(solution)/shard_map/ppermute | solution.py:494
  43.5 1.5 %collective-permute-done.mate_ref = f32[1024,128]{1,0:T(8,128)S(1)} collective-permute-done((f32[1024,128]{1,0:T(8,128)S(1)}, f32[1024,128]{1,0:T(8,128)S(1)}, u32[]{:S(2)}, u32[]{:S(2)}) %collective-permute-start) | collective-permute-done | bytes 524320 | tf_op jit(solution)/shard_map/ppermute | solution.py:494
  45.0 1.2 %shard_map.78 = (f32[8,8,256]{2,1,0:T(8,128)S(1)}, f32[2,64,128]{2,1,0:T(8,128)S(1)}) custom-call(f32[8,256]{1,0:T(8,128)S(1)} %get-tuple-element.18.own_ref, f32[8,256]{1,0:T(8,128)S(1)} %get-tuple-element.19.part_ref, f32[1024,128]{1,0:T(8,128)S(1)} %bitcast.14, f32[1024,128]{1,0:T(8,128)S(1)} %collective-permute-done.mate_ref, ...), custom_call_target="tpu_custom_call" | custom-call | tf_op jit(solution)/shard_map/pallas_call | solution.py:540
  46.2 9.4 %all_to_all.32.shares_ref = f32[8,8,256]{2,1,0:T(8,128)S(1)} all-to-all(f32[8,8,256]{2,1,0:T(8,128)S(1)} %get-tuple-element.25), channel_id=1, replica_groups=mesh['chip'=64,'core'=2,'rep'=4] {'core','rep'}, dimensions={0} | all-to-all | bytes 131072 | tf_op jit(solution)/shard_map/all_to_all | solution.py:490
  55.6 0.9 shard_map.79
  56.5 19.0 %all_to_all.33 = f32[320,2,128]{2,1,0:T(2,128)S(1)} all-to-all(f32[320,2,128]{2,1,0:T(2,128)S(1)} %bitcast.17), channel_id=1, replica_groups=mesh['chip'=64,'core'=2,'rep'=4] {'chip'}, dimensions={0} | all-to-all | bytes 655360 | tf_op jit(solution)/shard_map/all_to_all | solution.py:490
  75.5 1.0 shard_map.80
  76.5 10.0 %all_to_all.34 = f32[72,2,128]{2,1,0:T(2,128)S(1)} all-to-all(f32[72,2,128]{2,1,0:T(2,128)S(1)} %bitcast.19), channel_id=1, replica_groups=mesh['chip'=64,'core'=2,'rep'=4] {'core','rep'}, dimensions={0} | all-to-all | bytes 147456 | tf_op jit(solution)/shard_map/all_to_all | solution.py:490
  86.5 14.9 %all_to_all.35 = f32[64,1,128]{2,1,0:T(1,128)S(1)} all-to-all(f32[64,1,128]{2,1,0:T(1,128)S(1)} %bitcast.21), channel_id=1, replica_groups=mesh['chip'=64,'core'=2,'rep'=4] {'chip'}, dimensions={0} | all-to-all | bytes 65536 | tf_op jit(solution)/shard_map/all_to_all | solution.py:490
  101.4 0.7 shard_map.82
  (1 shorter events, 0.0 us)
Async XLA Ops:
  37.7 7.3 %collective-permute-start = (f32[1024,128]{1,0:T(8,128)S(1)}, f32[1024,128]{1,0:T(8,128)S(1)}, u32[]{:S(2)}, u32[]{:S(2)}) collective-permute-start(f32[1024,128]{1,0:T(8,128)S(1)} %bitcast.13), channel_id=1, source_target_pairs={{0,4},{4,0},{1,5},{5,1},{2,6},{6,2},{3,7},{7,3},{8,12},{12,8},{9,1... | collective-permute-start | bytes 1572872 | tf_op jit(solution)/shard_map/ppermute | solution.py:494

commit v7 on v6

--- a/solution.py
+++ b/solution.py
@@ -551,14 +551,14 @@
          floats(2 * blk_g, width)],
         info_scr + [cols_scr, wide_scr, half_scr, half_scr],
     )(shares, code, info, band, trans)
-    got = exchange(send.reshape(STEP * chips // 2, 2, LANES), "chip").reshape(send.shape)
+    got = exchange(send.reshape(chips, 1, STEP * LANES), "chip").reshape(send.shape)
     (share,) = call(
         third_kernel,
         [VMEM, VMEM, VMEM, VMEM, VMEM, ANY, VMEM, VMEM],
         [floats(2 * replicas * SHARE, LANES)],
         info_scr + [wide_scr, cols_scr, half_scr],
     )(code, got, ext, part, first, info, band, trans)
-    shares = exchange(share.reshape(replicas * SHARE, 2, LANES), LOCAL).reshape(share.shape)
+    shares = exchange(share.reshape(2 * replicas, 1, SHARE * LANES), LOCAL).reshape(share.shape)
     second, stats = call(
         stats_kernel, [VMEM, VMEM], [floats(2 * blk_g, LANES), floats(chips, LANES)]
     )(shares, first)

time: 102 us -> 102 us (level)
  no operation moved by 1% of the time
where the time goes in v7:
time: 102 us
  blocking collectives  86.6 us (85%)
  Pallas kernels  6.95 us (7%)
  starting transfers between devices  5.78 us (6%)
  waiting for transfers between devices  1.51 us (1%)
  between operations  1.32 us (1%)
    all_to_all x5, blocking collectives, exchange(): return lax.all_to_all(block, axis, 0, 0, tiled=True)  86.6 us
    ppermute x1, starting transfers between devices, swap_cores(): return lax.ppermute(block, 'core', [(0, 1), (1, 0)])  5.78 us
    pallas_call x1, Pallas kernels, shards(): pl.pallas_call(first_kernel, in_specs=[SMEM] + [HBM] * 5, out_shape=[jax....  3.1 us
  transfers between devices with their start and end apart: 1, of which 1 were waited for; matrix products, arithmetic and copies ran while one was open for 0% of the time, Pallas kernels for 0%

profile of v7, /device:TPU:1, one launch (start us, length us, event | category | flops | bytes accessed | tf_op | source)
XLA Modules:
  0.0 102.1 jit_solution(4612550774408450254)
XLA Ops:
  1.3 3.1 %shard_map.77 = (f32[8,256]{1,0:T(8,128)S(1)}, s32[24]{0:T(128)S(1)}, f32[1024,128]{1,0:T(8,128)S(1)}, f32[8,256]{1,0:T(8,128)S(1)}, f32[2,5,256,256]{3,2,1,0:T(8,128)S(1)}, /*index=5*/f32[6,256,256]{2,1,0:T(8,128)S(1)}) custom-call(s32[1]{0:T(128)S(6)} %copy.12.count_ref, s32[16,128]{1,0:T(8,128)} %bitcast.22, s32[6]{0:T(128)} %cols_in.1, s32[6]{0:T(128)} %rows_in.1, ...), custom_call_target="tpu_custom_call" | custom-call | tf_op jit(solution)/shard_map/pallas_call | solution.py:516
  4.4 33.3 %all_to_all.31 = f32[64,1,2048]{2,1,0:T(1,128)S(1)} all-to-all(f32[64,1,2048]{2,1,0:T(1,128)S(1)} %bitcast.16), channel_id=1, replica_groups=mesh['chip'=64,'core'=2,'rep'=4] {'chip'}, dimensions={0} | all-to-all | bytes 1048576 | tf_op jit(solution)/shard_map/all_to_all | solution.py:490
  37.7 5.8 %collective-permute-start = (f32[1024,128]{1,0:T(8,128)S(1)}, f32[1024,128]{1,0:T(8,128)S(1)}, u32[]{:S(2)}, u32[]{:S(2)}) collective-permute-start(f32[1024,128]{1,0:T(8,128)S(1)} %bitcast.13), channel_id=1, source_target_pairs={{0,4},{4,0},{1,5},{5,1},{2,6},{6,2},{3,7},{7,3},{8,12},{12,8},{9,1... | collective-permute-start | bytes 1572872 | tf_op jit(solution)/shard_map/ppermute | solution.py:494
  43.5 1.5 %collective-permute-done.mate_ref = f32[1024,128]{1,0:T(8,128)S(1)} collective-permute-done((f32[1024,128]{1,0:T(8,128)S(1)}, f32[1024,128]{1,0:T(8,128)S(1)}, u32[]{:S(2)}, u32[]{:S(2)}) %collective-permute-start) | collective-permute-done | bytes 524320 | tf_op jit(solution)/shard_map/ppermute | solution.py:494
  45.0 1.2 %shard_map.78 = (f32[8,8,256]{2,1,0:T(8,128)S(1)}, f32[2,64,128]{2,1,0:T(8,128)S(1)}) custom-call(f32[8,256]{1,0:T(8,128)S(1)} %get-tuple-element.18.own_ref, f32[8,256]{1,0:T(8,128)S(1)} %get-tuple-element.19.part_ref, f32[1024,128]{1,0:T(8,128)S(1)} %bitcast.14, f32[1024,128]{1,0:T(8,128)S(1)} %collective-permute-done.mate_ref, ...), custom_call_target="tpu_custom_call" | custom-call | tf_op jit(solution)/shard_map/pallas_call | solution.py:540
  46.2 9.4 %all_to_all.32.shares_ref = f32[8,8,256]{2,1,0:T(8,128)S(1)} all-to-all(f32[8,8,256]{2,1,0:T(8,128)S(1)} %get-tuple-element.25), channel_id=1, replica_groups=mesh['chip'=64,'core'=2,'rep'=4] {'core','rep'}, dimensions={0} | all-to-all | bytes 131072 | tf_op jit(solution)/shard_map/all_to_all | solution.py:490
  55.6 0.9 shard_map.79
  56.5 19.0 %all_to_all.33 = f32[64,1,1280]{2,1,0:T(1,128)S(1)} all-to-all(f32[64,1,1280]{2,1,0:T(1,128)S(1)} %bitcast.17), channel_id=1, replica_groups=mesh['chip'=64,'core'=2,'rep'=4] {'chip'}, dimensions={0} | all-to-all | bytes 655360 | tf_op jit(solution)/shard_map/all_to_all | solution.py:490
  75.5 1.0 shard_map.80
  76.5 10.0 %all_to_all.34 = f32[8,1,2304]{2,1,0:T(1,128)S(1)} all-to-all(f32[8,1,2304]{2,1,0:T(1,128)S(1)} %bitcast.19), channel_id=1, replica_groups=mesh['chip'=64,'core'=2,'rep'=4] {'core','rep'}, dimensions={0} | all-to-all | bytes 147456 | tf_op jit(solution)/shard_map/all_to_all | solution.py:490
  86.5 14.9 %all_to_all.35 = f32[64,1,128]{2,1,0:T(1,128)S(1)} all-to-all(f32[64,1,128]{2,1,0:T(1,128)S(1)} %bitcast.21), channel_id=1, replica_groups=mesh['chip'=64,'core'=2,'rep'=4] {'chip'}, dimensions={0} | all-to-all | bytes 65536 | tf_op jit(solution)/shard_map/all_to_all | solution.py:490
  101.4 0.7 shard_map.82
  (1 shorter events, 0.0 us)
Async XLA Ops:
  37.7 7.3 %collective-permute-start = (f32[1024,128]{1,0:T(8,128)S(1)}, f32[1024,128]{1,0:T(8,128)S(1)}, u32[]{:S(2)}, u32[]{:S(2)}) collective-permute-start(f32[1024,128]{1,0:T(8,128)S(1)} %bitcast.13), channel_id=1, source_target_pairs={{0,4},{4,0},{1,5},{5,1},{2,6},{6,2},{3,7},{7,3},{8,12},{12,8},{9,1... | collective-permute-start | bytes 1572872 | tf_op jit(solution)/shard_map/ppermute | solution.py:494
